TPU v7x, 256 devices: a whole 4x4x8 slice. The times are simulated.
256 devices in a mesh: ctx: 32 (over x, z), head: 8 (over y, core).
Axes of the slice: x: 4, y: 4, z: 8, core: 2. Of those that a mesh axis runs over, the one named last changes fastest.
Arguments:
- query: bfloat16 [65536, 8192], P(('ctx', 'head')), as said below
- key: bfloat16 [65536, 1024], P(('ctx', 'head')), as said below
- value: bfloat16 [65536, 1024], P(('ctx', 'head')), may hold values from -6 to 6
- doc_ids: int32 [512], replicated, may hold values from 0 to 84, never falling along the last dimension, each value on 1 to 8 neighbouring positions
- plan: int32 [512], replicated, may hold values from 0 to 511, as said below
Outputs:
- attended: bfloat16 [65536, 8192], P('ctx', 'head')
Inputs may be any that keep to these rules, and one draw needn't show every extreme that they name: `doc_ids`: block ids never fall; each document holds 1 to 8 blocks, one exactly 8. `plan`: A permutation of the 512 blocks. Output positions k * 16 to (k + 1) * 16 - 1 belong to context shard k. Every shard receives 16 blocks; of the blocks j * 16 to (j + 1) * 16 - 1 at most 1 go to one shard, and exactly 1 to some shard. `query`: real values; no structure promised. `key`: real values; no structure promised.
All inputs are finite; a program needn't handle non-finite values.
Results may differ from a plain program's by a relative error of at most 0.0038.
Values may be sent and summed in bfloat16 or wider, within the bound.
No kernel may reach another device: no remote copies, remote signals or barrier semaphores. Data moves between devices by JAX's collectives and lax.ppermute only.
A program may use at most 128 MiB of HBM per device.

v0:
```python
import functools
import math

import jax
import jax.numpy as jnp
from jax import lax
from jax.experimental import pallas as pl
from jax.experimental.pallas import tpu as pltpu
from jax.sharding import PartitionSpec as P

HD = 128
BLK = 128
MAXDOC = 8
VMEM_BYTES = 60 * 1024 * 1024
SHARED_VMEM_BYTES = 32 * 1024 * 1024
HALO = MAXDOC - 1
CHUNKS = (2, 6)
EXP2_SCALE = math.log2(math.e) / math.sqrt(HD)


def attend_kernel(doc_ref, slot_ref, order_ref, shard_ref, *refs, heads, count, base, steps, ahead, paired, q_views):
    given, (out_ref, win_ref, held_ref, mixed_ref, kv_sems, q_sems, out_sems) = refs[:-7], refs[-7:]
    width = heads * HD
    own_ref = given[0]

    def copy_own():
        rows = (base + steps) * BLK
        return pltpu.make_async_copy(
            own_ref.at[pl.ds(0, rows), pl.ds(0, 2 * HD)], win_ref.at[pl.ds(ahead * BLK, rows)], kv_sems.at[0]
        )

    def copy_halo():
        return pltpu.make_async_copy(given[1], win_ref.at[pl.ds(0, ahead * BLK)], kv_sems.at[1])

    def copy_out(step):
        return pltpu.make_async_copy(
            mixed_ref.at[step], out_ref.at[slot_ref[base + step]], out_sems.at[step]
        )

    copy_own().start()
    if ahead:
        copy_halo().start()
    for view in range(steps):
        which, lead, row, column = q_views[view]
        source = given[which] if lead is None else given[which].at[lead]
        step = order_ref[view]
        pltpu.make_async_copy(
            source.at[pl.ds(row, BLK), pl.ds(column, width)], held_ref.at[step], q_sems.at[step]
        ).start()

    row = lax.broadcasted_iota(jnp.int32, (heads * BLK, BLK), 0) % BLK
    column = lax.broadcasted_iota(jnp.int32, (heads * BLK, BLK), 1)
    causal = column <= row
    copy_own().wait()
    if ahead:
        copy_halo().wait()

    lanes = 2 if paired else 1

    def per_turn(turn, _):
        at = lanes * turn
        first = base + at
        block = shard_ref[0] * count + first
        doc = doc_ref[block]
        tiles = jnp.int32(1)
        for back in range(1, MAXDOC):
            before = jnp.maximum(block - back, 0)
            tiles += jnp.where((block >= back) & (doc_ref[before] == doc), 1, 0)
        for lane in range(lanes):
            held = held_ref.at[at + lane]
            pltpu.make_async_copy(held, held, q_sems.at[at + lane]).wait()

        def with_tiles(tiles_of):
            windows = []
            for lane, n in enumerate(tiles_of):
                start = pl.multiple_of((first + lane + ahead + 1 - n) * BLK, BLK)
                windows.append(pl.ds(start, n * BLK))
            scores = []
            for lane, n in enumerate(tiles_of):
                queries = jnp.concatenate(
                    [held_ref[at + lane, :, head * HD : (head + 1) * HD] for head in range(heads)], axis=0
                )
                scores.append(lax.dot_general(
                    queries, win_ref[windows[lane], :HD], (((1,), (1,)), ((), ())),
                    preferred_element_type=jnp.float32,
                ))
            for lane, n in enumerate(tiles_of):
                last = jnp.where(causal, scores[lane][:, (n - 1) * BLK :], -jnp.inf)
                scores[lane] = (
                    last if n == 1 else jnp.concatenate([scores[lane][:, : (n - 1) * BLK], last], axis=1)
                )
            tops = [jnp.max(s, axis=1, keepdims=True) for s in scores]
            expos = [jnp.exp2((s - top) * EXP2_SCALE) for s, top in zip(scores, tops)]
            totals = [jnp.sum(e, axis=1, keepdims=True) for e in expos]
            sums = [
                jnp.dot(e.astype(jnp.bfloat16), win_ref[window, HD:], preferred_element_type=jnp.float32)
                for e, window in zip(expos, windows)
            ]
            for lane in range(len(tiles_of)):
                mixed = (sums[lane] / totals[lane]).astype(jnp.bfloat16)
                for head in range(heads):
                    mixed_ref[at + lane, :, head * HD : (head + 1) * HD] = mixed[head * BLK : (head + 1) * BLK]

        if paired:
            same = doc_ref[block + 1] == doc
            for n in range(1, MAXDOC + 1):
                if n < MAXDOC:
                    pl.when((tiles == n) & same)(functools.partial(with_tiles, (n, n + 1)))
                pl.when((tiles == n) & jnp.logical_not(same))(functools.partial(with_tiles, (n, 1)))
        else:
            for n in range(1, MAXDOC + 1):
                pl.when(tiles == n)(functools.partial(with_tiles, (n,)))
        for lane in range(lanes):
            copy_out(at + lane).start()
        return 0

    lax.fori_loop(0, steps // lanes, per_turn, 0)
    for step in range(steps):
        copy_out(step).wait()


def attend(own, halo, sources, q_views, order, heads, tables, count, slots, base=0, steps=None, result=None):
    doc_ids, slot, shard = tables
    steps = count if steps is None else steps
    width = heads * HD
    ahead = 0 if halo is None else HALO
    alone = steps < count
    given = [own] + ([] if halo is None else [halo])
    views = [(len(given) + which if which >= 0 else 0, lead, row, column) for which, lead, row, column in q_views]
    given = given + list(sources) + ([] if result is None else [result])
    smem, anywhere = pl.BlockSpec(memory_space=pltpu.SMEM), pl.BlockSpec(memory_space=pl.ANY)
    return pl.pallas_call(
        functools.partial(
            attend_kernel, heads=heads, count=count, base=base, steps=steps, ahead=ahead, paired=alone,
            q_views=views
        ),
        in_specs=[smem] * 4 + [anywhere] * len(given),
        out_specs=pl.BlockSpec(memory_space=pl.ANY),
        out_shape=jax.ShapeDtypeStruct((slots, BLK, width), jnp.bfloat16),
        scratch_shapes=[
            pltpu.VMEM(((base + steps + ahead) * BLK, 2 * HD), jnp.bfloat16),
            pltpu.VMEM((steps, BLK, width), jnp.bfloat16),
            pltpu.VMEM((steps, BLK, width), jnp.bfloat16),
            pltpu.SemaphoreType.DMA((2,)),
            pltpu.SemaphoreType.DMA((steps,)),
            pltpu.SemaphoreType.DMA((steps,)),
        ],
        input_output_aliases={} if result is None else {4 + len(given) - 1: 0},
        compiler_params=pltpu.CompilerParams(vmem_limit_bytes=VMEM_BYTES if alone else SHARED_VMEM_BYTES),
        cost_estimate=pl.CostEstimate(
            flops=10**12 if ahead else 0, bytes_accessed=0, transcendentals=0
        ),
        name="attend",
    )(doc_ids, slot, order, shard, *given)


def first_parts_kernel(k_ref, v_ref, q_ref, out_ref, held_ref, in_sems, out_sems, *, head_count, width):
    kv_width, q_width = k_ref.shape[1] // head_count, q_ref.shape[1] // head_count
    rows = q_ref.shape[0]

    def fetches(h):
        pieces = (
            (k_ref, h * kv_width, 0, kv_width),
            (v_ref, h * kv_width, kv_width, kv_width),
            (q_ref, h * q_width, 2 * kv_width, width),
        )
        return [
            pltpu.make_async_copy(
                ref.at[:, pl.ds(at, size)], held_ref.at[h, :, pl.ds(to, size)], in_sems.at[h, i]
            )
            for i, (ref, at, to, size) in enumerate(pieces)
        ]

    def store(h):
        return pltpu.make_async_copy(held_ref.at[h], out_ref.at[h], out_sems.at[h])

    for h in range(head_count):
        for fetch in fetches(h):
            fetch.start()
    for h in range(head_count):
        for fetch in fetches(h):
            fetch.wait()
        store(h).start()
    for h in range(head_count):
        store(h).wait()


def first_parts(key, value, query, head_count, width):
    shape = (head_count, query.shape[0], 2 * key.shape[1] // head_count + width)
    return pl.pallas_call(
        functools.partial(first_parts_kernel, head_count=head_count, width=width),
        in_specs=[pl.BlockSpec(memory_space=pl.ANY)] * 3,
        out_specs=pl.BlockSpec(memory_space=pl.ANY),
        out_shape=jax.ShapeDtypeStruct(shape, jnp.bfloat16),
        scratch_shapes=[
            pltpu.VMEM(shape, jnp.bfloat16),
            pltpu.SemaphoreType.DMA((head_count, 3)),
            pltpu.SemaphoreType.DMA((head_count,)),
        ],
        compiler_params=pltpu.CompilerParams(vmem_limit_bytes=VMEM_BYTES),
        name="first_parts",
    )(key, value, query)


def later_parts_kernel(place_ref, q_ref, *refs, chips, firsts, widths):
    chunks = len(widths)
    in_sems, out_sems = refs[-2:]
    held_refs, out_refs = refs[-2 - chunks : -2], refs[: -2 - chunks]
    core, chip = place_ref[0], place_ref[1]
    q_width = q_ref.shape[1] // (2 * chips)
    moves = []
    for chunk, (first, width) in enumerate(zip(firsts, widths)):
        outs = out_refs[chunk * (chips + 1) : (chunk + 1) * (chips + 1)]
        for side in range(2):
            for step in range(chips):
                member = lax.rem(chip + step, chips) * 2 + lax.rem(core + side, 2)
                column = pl.multiple_of(member * q_width + first, HD)
                held = held_refs[chunk].at[side * chips + step]
                at = (chunk * 2 + side) * chips + step
                out = outs[chips].at[step] if side else outs[step].at[0]
                moves.append((
                    pltpu.make_async_copy(q_ref.at[:, pl.ds(column, width)], held, in_sems.at[at]),
                    pltpu.make_async_copy(held, out, out_sems.at[at]),
                ))
    for fetch, _ in moves:
        fetch.start()
    for fetch, store in moves:
        fetch.wait()
        store.start()
    for _, store in moves:
        store.wait()


def later_parts(query, place, head_count, firsts, widths):
    rows, chips = query.shape[0], head_count // 2
    shapes = []
    for width in widths:
        shapes += [jax.ShapeDtypeStruct((2, rows, width), jnp.bfloat16)] * chips
        shapes.append(jax.ShapeDtypeStruct((chips, rows, width), jnp.bfloat16))
    copies = 2 * chips * len(widths)
    outs = pl.pallas_call(
        functools.partial(later_parts_kernel, chips=chips, firsts=firsts, widths=widths),
        in_specs=[pl.BlockSpec(memory_space=pltpu.SMEM), pl.BlockSpec(memory_space=pl.ANY)],
        out_specs=[pl.BlockSpec(memory_space=pl.ANY)] * len(shapes),
        out_shape=shapes,
        scratch_shapes=[pltpu.VMEM((2 * chips, rows, width), jnp.bfloat16) for width in widths]
        + [pltpu.SemaphoreType.DMA((copies,))] * 2,
        compiler_params=pltpu.CompilerParams(vmem_limit_bytes=VMEM_BYTES),
        cost_estimate=pl.CostEstimate(flops=0, bytes_accessed=4 * query.size, transcendentals=0),
        name="later_parts",
    )(place, query)
    split = [outs[(chips + 1) * i : (chips + 1) * (i + 1)] for i in range(len(widths))]
    return [list(part[:chips]) for part in split], [part[chips] for part in split]


def fill_kernel(got_ref, *refs):
    held_ref, in_sems, out_sems = refs[-3:]
    steps = held_ref.shape[0]
    out_refs = refs[steps : 2 * steps]
    fetches = [pltpu.make_async_copy(got_ref.at[i], held_ref.at[i], in_sems.at[i]) for i in range(steps)]
    stores = [pltpu.make_async_copy(held_ref.at[i], out_refs[i].at[1], out_sems.at[i]) for i in range(steps)]
    for fetch in fetches:
        fetch.start()
    for fetch, store in zip(fetches, stores):
        fetch.wait()
        store.start()
    for store in stores:
        store.wait()


def fill(parts, got):
    return pl.pallas_call(
        fill_kernel,
        in_specs=[pl.BlockSpec(memory_space=pl.ANY)] * (1 + len(parts)),
        out_specs=[pl.BlockSpec(memory_space=pl.ANY)] * len(parts),
        out_shape=[jax.ShapeDtypeStruct(part.shape, part.dtype) for part in parts],
        scratch_shapes=[pltpu.VMEM(got.shape, got.dtype)] + [pltpu.SemaphoreType.DMA((len(parts),))] * 2,
        input_output_aliases={1 + i: i for i in range(len(parts))},
        compiler_params=pltpu.CompilerParams(vmem_limit_bytes=VMEM_BYTES),
        cost_estimate=pl.CostEstimate(flops=0, bytes_accessed=0, transcendentals=0),
        name="fill",
    )(got, *parts)


def place_kernel(source_ref, *refs, count, first, width):
    received_ref, out_ref, held_ref, in_sems, out_sems = refs[0], refs[-4], refs[-3], refs[-2], refs[-1]

    def fetch(i):
        return pltpu.make_async_copy(received_ref.at[source_ref[i]], held_ref.at[i], in_sems.at[i])

    def store(i):
        return pltpu.make_async_copy(
            held_ref.at[i], out_ref.at[pl.ds(i * BLK, BLK), pl.ds(first, width)], out_sems.at[i]
        )

    for i in range(count):
        fetch(i).start()
    for i in range(count):
        fetch(i).wait()
        store(i).start()
    for i in range(count):
        store(i).wait()


def place(received, source, result, first, count, full_width):
    slots, _, width = received.shape
    given = [received] if result is None else [received, result]
    return pl.pallas_call(
        functools.partial(place_kernel, count=count, first=first, width=width),
        in_specs=[pl.BlockSpec(memory_space=pltpu.SMEM)] + [pl.BlockSpec(memory_space=pl.ANY)] * len(given),
        out_specs=pl.BlockSpec(memory_space=pl.ANY),
        out_shape=jax.ShapeDtypeStruct((count * BLK, full_width), jnp.bfloat16),
        scratch_shapes=[
            pltpu.VMEM((count, BLK, width), jnp.bfloat16),
            pltpu.SemaphoreType.DMA((count,)),
            pltpu.SemaphoreType.DMA((count,)),
        ],
        input_output_aliases={} if result is None else {2: 0},
        compiler_params=pltpu.CompilerParams(vmem_limit_bytes=SHARED_VMEM_BYTES),
        cost_estimate=pl.CostEstimate(flops=0, bytes_accessed=4 * count * BLK * width, transcendentals=0),
        name="place",
    )(source, *given)


def shards(query, key, value, doc_ids, plan):
    head_count = lax.axis_size("head")
    shard_count = lax.axis_size("ctx")
    local_rows = query.shape[0]
    rows = head_count * local_rows
    count = rows // BLK
    per_device = local_rows // BLK
    q_width = query.shape[1] // head_count
    shard = lax.axis_index("ctx").astype(jnp.int32)
    member = lax.axis_index("head").astype(jnp.int32)
    core, chip, chips = member % 2, member // 2, head_count // 2

    widths = [heads * HD for heads in CHUNKS]
    firsts = [sum(widths[:i]) for i in range(len(widths))]
    opening = first_parts(key, value, query, head_count, widths[0])
    kept, given = later_parts(query, jnp.stack([core, chip]), head_count, firsts[1:], widths[1:])
    swap = [(h, h ^ 1) for h in range(head_count)]
    later = [fill(parts, lax.ppermute(part, "head", swap)) for parts, part in zip(kept, given)]
    opening = lax.all_to_all(opening, "head", split_axis=0, concat_axis=0, tiled=True)

    index = jnp.arange(count, dtype=jnp.int32)
    own_ids = shard * count + index
    position = jnp.arange(plan.shape[0], dtype=jnp.int32)
    target = jnp.sum(
        jnp.where(plan[None, :] == own_ids[:, None], position[None, :] // count, 0), axis=1, dtype=jnp.int32
    )
    source = lax.dynamic_slice_in_dim(plan, shard * count, count) // count
    step_of, rest = index // (2 * per_device), index % (2 * per_device)
    giver = (chip - step_of + chips) % chips * 2 + (core + rest // per_device) % 2
    arrival = giver * per_device + rest % per_device

    opening, later, target, source, arrival = lax.optimization_barrier(
        (opening, later, target, source, arrival)
    )
    opening = opening.reshape(rows, 2 * HD + widths[0])
    halo = lax.ppermute(
        opening[rows - HALO * BLK :, : 2 * HD], "ctx", [(i, i + 1) for i in range(shard_count - 1)]
    )
    tables = (doc_ids, target, shard.reshape(1))

    result = None
    for turn, heads in enumerate(CHUNKS):
        if turn == 0:
            views = [(-1, None, i * BLK, 2 * HD) for i in range(count)]
            sent = attend(
                opening, None, [], views[MAXDOC:], index, heads, tables, count, shard_count, MAXDOC, count - MAXDOC
            )
            sent = attend(
                opening, halo, [], views[:MAXDOC], index, heads, tables, count, shard_count, 0, MAXDOC, sent
            )
        else:
            sources = []
            for step, part in enumerate(later[turn - 1]):
                onward = [(h, (h + 2 * step) % head_count) for h in range(head_count)]
                sources.append(lax.ppermute(part, "head", onward) if step else part)
            views = [
                (i // (2 * per_device), i // per_device % 2, i % per_device * BLK, 0) for i in range(count)
            ]
            sent = attend(opening, halo, sources, views, arrival, heads, tables, count, shard_count)
        received = lax.all_to_all(sent, "ctx", split_axis=0, concat_axis=0, tiled=True)
        result = place(received, source, result, firsts[turn], count, q_width)
    return result


def solution(mesh):
    return jax.shard_map(
        shards,
        mesh=mesh,
        in_specs=(
            P(("ctx", "head"), None),
            P(("ctx", "head"), None),
            P(("ctx", "head"), None),
            P(),
            P(),
        ),
        out_specs=P("ctx", "head"),
        check_vma=False,
    )
```

profile of v0, /device:TPU:33, one launch (start us, length us, event | category | flops | bytes accessed | tf_op | source)
XLA Modules:
  0.0 266.6 jit_solution(4340034194924778531)
XLA Ops:
  0.0 2.6 first_parts.1
  2.6 5.2 %all-to-all-start = ((bf16[8,256,512]{2,1,0:T(8,128)(2,1)}), bf16[8,256,512]{2,1,0:T(8,128)(2,1)S(1)}, u32[]{:S(2)}, u32[]{:S(2)}) async-start(bf16[8,256,512]{2,1,0:T(8,128)(2,1)} %first_parts.1), calls=%async_computation | async-start | bytes 4194304 | tf_op jit(solution)/shard_map/all_to_all | solution.py:343
  7.8 0.6 pad_add_fusion.place_ref
  8.4 0.0 copy-start.8
  8.4 3.6 %later_parts.1 = (bf16[2,256,768]{2,1,0:T(8,128)(2,1)}, bf16[2,256,768]{2,1,0:T(8,128)(2,1)}, bf16[2,256,768]{2,1,0:T(8,128)(2,1)}, bf16[2,256,768]{2,1,0:T(8,128)(2,1)}, bf16[4,256,768]{2,1,0:T(8,128)(2,1)}) custom-call(s32[2]{0:T(128)} %pad_add_fusion.place_ref, bf16[256,8192]{1,0:T(8,128)(2,1)} %q_ref.3), custom_call_target="tpu_custom_call" | custom-call | bytes 8388608 | tf_op jit(solution)/shard_map/later_parts/pallas_call | solution.py:241
  12.0 0.1 collective-permute-start
  12.1 0.0 copy-done.8
  12.1 0.1 and_select_fusion.6
  12.2 0.7 select_reduce_fusion.slot_ref
  12.9 3.0 %collective-permute-done.got_ref = bf16[4,256,768]{2,1,0:T(8,128)(2,1)} collective-permute-done((bf16[4,256,768]{2,1,0:T(8,128)(2,1)}, bf16[4,256,768]{2,1,0:T(8,128)(2,1)}, u32[]{:S(2)}, u32[]{:S(2)}) %collective-permute-start) | collective-permute-done | bytes 1572896 | tf_op jit(solution)/shard_map/ppermute | solution.py:342
  15.8 2.2 fill.1
  18.1 16.1 %all-to-all-done = bf16[8,256,512]{2,1,0:T(8,128)(2,1)S(1)} async-done(((bf16[8,256,512]{2,1,0:T(8,128)(2,1)}), bf16[8,256,512]{2,1,0:T(8,128)(2,1)S(1)}, u32[]{:S(2)}, u32[]{:S(2)}) %all-to-all-start) | async-done | bytes 2097184 | tf_op jit(solution)/shard_map/all_to_all | solution.py:343
  34.1 0.0 copy-start
  34.2 3.5 %collective-permute-start.1 = (bf16[896,256]{1,0:T(8,128)(2,1)S(1)}, bf16[896,256]{1,0:T(8,128)(2,1)S(1)}, u32[]{:S(2)}, u32[]{:S(2)}) collective-permute-start(bf16[896,256]{1,0:T(8,128)(2,1)S(1)} %slice.4), channel_id=1, source_target_pairs={{0,8},{8,16},{16,24},{24,32},{32,40},{40,48},{48,56},{56,64},{64,7... | collective-permute-start | bytes 1376264 | tf_op jit(solution)/shard_map/ppermute | solution.py:360
  37.7 0.4 collective-permute-start.2
  38.1 1.8 collective-permute-start.3
  39.9 0.7 collective-permute-start.4
  40.6 0.5 iota.24.order_ref
  41.1 0.0 copy-done
  41.1 6.2 %attend.4.refs_2_ = bf16[32,128,256]{2,1,0:T(8,128)(2,1)} custom-call(s32[512]{0:T(512)} %doc_ref.5, s32[16]{0:T(128)} %select_reduce_fusion.slot_ref, s32[16]{0:T(128)} %iota.24.order_ref, s32[1]{0:T(128)} %bitcast.2.shard_ref, bf16[2048,512]{1,0:T(8,128)(2,1)} %bitcast.5), custom_call_target="tpu_custom_call" | custom-call | tf_op jit(solution)/shard_map/attend/pallas_call | solution.py:132
  47.2 0.1 collective-permute-done.1.refs_1_
  47.3 0.0 copy-start.6
  47.3 0.6 iota.23.order_ref
  48.0 0.2 copy-done.6
  48.1 5.6 %attend.5 = bf16[32,128,256]{2,1,0:T(8,128)(2,1)} custom-call(s32[512]{0:T(512)} %doc_ref.5, s32[16]{0:T(128)} %select_reduce_fusion.slot_ref, s32[16]{0:T(128)} %iota.23.order_ref, s32[1]{0:T(128)} %bitcast.2.shard_ref, bf16[2048,512]{1,0:T(8,128)(2,1)} %bitcast.6, bf16[896,256]{1,0:T(8,128)(2,1)} %copy-done.6, ...), custom_call_target="tpu_custom_call", output_to_operand_aliasing={{}: (6, {})} | custom-call | flops 999999995904 | tf_op jit(solution)/shard_map/attend/pallas_call | solution.py:132
  53.7 0.0 copy-start.1
  53.7 0.0 copy-start.3
  53.8 0.0 copy-start.4
  53.8 0.0 copy-start.5
  53.8 0.0 copy-start.7
  53.8 12.3 %all-to-all-start.2 = ((bf16[32,128,256]{2,1,0:T(8,128)(2,1)}), bf16[32,128,256]{2,1,0:T(8,128)(2,1)}, u32[]{:S(2)}, u32[]{:S(2)}) async-start(bf16[32,128,256]{2,1,0:T(8,128)(2,1)} %attend.5), calls=%async_computation.2 | async-start | bytes 4194304 | tf_op jit(solution)/shard_map/all_to_all | solution.py:384
  66.1 0.0 collective-permute-done.2.refs_3_
  66.1 7.4 %collective-permute-done.3.refs_4_ = bf16[2,256,768]{2,1,0:T(8,128)(2,1)} collective-permute-done((bf16[2,256,768]{2,1,0:T(8,128)(2,1)}, bf16[2,256,768]{2,1,0:T(8,128)(2,1)}, u32[]{:S(2)}, u32[]{:S(2)}) %collective-permute-start.3) | collective-permute-done | bytes 786464 | tf_op jit(solution)/shard_map/ppermute | solution.py:379
  73.5 1.3 collective-permute-done.4.refs_5_
  74.8 0.0 copy-done.1
  74.8 0.0 copy-done.3
  74.8 0.0 copy-done.4
  74.8 0.0 copy-done.5
  74.8 0.0 copy-done.7
  74.8 23.4 %attend.3 = bf16[32,128,768]{2,1,0:T(8,128)(2,1)S(1)} custom-call(s32[512]{0:T(512)S(1)} %copy-done.4, s32[16]{0:T(128)S(1)} %copy-done.5, s32[16]{0:T(128)S(1)} %get-tuple-element.33.order_ref, s32[1]{0:T(128)} %bitcast.2.shard_ref, bf16[2048,512]{1,0:T(8,128)(2,1)S(1)} %bitcast.7, bf16[896,256]{1,0:T(8,128)(2,1)S(1)} %copy-done.7, ...), custom_call_target="tpu_custom_call" | custom-call | flops 999999995904 | tf_op jit(solution)/shard_map/attend/pallas_call | solution.py:132
  98.2 0.0 copy-start.2
  98.2 2.7 copy-done.2
  100.9 14.3 %all-to-all-done.2.refs_0_ = bf16[32,128,256]{2,1,0:T(8,128)(2,1)} async-done(((bf16[32,128,256]{2,1,0:T(8,128)(2,1)}), bf16[32,128,256]{2,1,0:T(8,128)(2,1)}, u32[]{:S(2)}, u32[]{:S(2)}) %all-to-all-start.2) | async-done | bytes 2097184 | tf_op jit(solution)/shard_map/all_to_all | solution.py:384
  115.2 6.6 %all-to-all-start.1 = ((bf16[32,128,768]{2,1,0:T(8,128)(2,1)}), bf16[32,128,768]{2,1,0:T(8,128)(2,1)}, u32[]{:S(2)}, u32[]{:S(2)}) async-start(bf16[32,128,768]{2,1,0:T(8,128)(2,1)} %copy-done.2), calls=%async_computation.1 | async-start | bytes 12582912 | tf_op jit(solution)/shard_map/all_to_all | solution.py:384
  121.9 2.7 %place.2.refs_1_ = bf16[2048,1024]{1,0:T(8,128)(2,1)} custom-call(s32[16]{0:T(128)S(1)} %get-tuple-element.31.source_ref, bf16[32,128,256]{2,1,0:T(8,128)(2,1)} %all-to-all-done.2.refs_0_), custom_call_target="tpu_custom_call" | custom-call | bytes 2097152 | tf_op jit(solution)/shard_map/place/pallas_call | solution.py:308
  124.6 138.1 %all-to-all-done.1.refs_0_ = bf16[32,128,768]{2,1,0:T(8,128)(2,1)} async-done(((bf16[32,128,768]{2,1,0:T(8,128)(2,1)}), bf16[32,128,768]{2,1,0:T(8,128)(2,1)}, u32[]{:S(2)}, u32[]{:S(2)}) %all-to-all-start.1) | async-done | bytes 6291488 | tf_op jit(solution)/shard_map/all_to_all | solution.py:384
  262.7 3.7 %place.3 = bf16[2048,1024]{1,0:T(8,128)(2,1)} custom-call(s32[16]{0:T(128)S(1)} %get-tuple-element.31.source_ref, bf16[32,128,768]{2,1,0:T(8,128)(2,1)} %all-to-all-done.1.refs_0_, bf16[2048,1024]{1,0:T(8,128)(2,1)} %place.2.refs_1_), custom_call_target="tpu_custom_call", output_to_operand_aliasing={{}: (2, {})} | custom-call | bytes 6291456 | tf_op jit(solution)/shard_map/place/pallas_call | solution.py:308
  (3 shorter events, 0.0 us)
Async XLA Ops:
  2.6 31.5 %all-to-all-start = ((bf16[8,256,512]{2,1,0:T(8,128)(2,1)}), bf16[8,256,512]{2,1,0:T(8,128)(2,1)S(1)}, u32[]{:S(2)}, u32[]{:S(2)}) async-start(bf16[8,256,512]{2,1,0:T(8,128)(2,1)} %first_parts.1), calls=%async_computation | async-start | bytes 4194304 | tf_op jit(solution)/shard_map/all_to_all | solution.py:343
  8.4 3.7 %copy-start.8 = (s32[512]{0:T(512)S(1)}, s32[512]{0:T(512)}, u32[]{:S(2)}) copy-start(s32[512]{0:T(512)} %param.9) | copy-start | bytes 6148
  12.0 3.8 %collective-permute-start = (bf16[4,256,768]{2,1,0:T(8,128)(2,1)}, bf16[4,256,768]{2,1,0:T(8,128)(2,1)}, u32[]{:S(2)}, u32[]{:S(2)}) collective-permute-start(bf16[4,256,768]{2,1,0:T(8,128)(2,1)} %get-tuple-element.22), channel_id=1, source_target_pairs={{0,1},{1,0},{2,3},{3,2},{4,5},{5,4},{6,7},{7,6},{8,9},{9,8},{10,11... | collective-permute-start | bytes 4718600 | tf_op jit(solution)/shard_map/ppermute | solution.py:342
  34.1 6.9 %copy-start = (bf16[8,256,512]{2,1,0:T(8,128)(2,1)}, bf16[8,256,512]{2,1,0:T(8,128)(2,1)S(1)}, u32[]{:S(2)}) copy-start(bf16[8,256,512]{2,1,0:T(8,128)(2,1)S(1)} %all-to-all-done) | copy-start | bytes 6291460
  34.2 13.2 %collective-permute-start.1 = (bf16[896,256]{1,0:T(8,128)(2,1)S(1)}, bf16[896,256]{1,0:T(8,128)(2,1)S(1)}, u32[]{:S(2)}, u32[]{:S(2)}) collective-permute-start(bf16[896,256]{1,0:T(8,128)(2,1)S(1)} %slice.4), channel_id=1, source_target_pairs={{0,8},{8,16},{16,24},{24,32},{32,40},{40,48},{48,56},{56,64},{64,7... | collective-permute-start | bytes 1376264 | tf_op jit(solution)/shard_map/ppermute | solution.py:360
  37.7 28.4 %collective-permute-start.2 = (bf16[2,256,768]{2,1,0:T(8,128)(2,1)}, bf16[2,256,768]{2,1,0:T(8,128)(2,1)}, u32[]{:S(2)}, u32[]{:S(2)}) collective-permute-start(bf16[2,256,768]{2,1,0:T(8,128)(2,1)} %get-tuple-element.36), channel_id=1, source_target_pairs={{0,2},{1,3},{2,4},{3,5},{4,6},{5,7},{6,0},{7,1},{8,10},{9,11},{10,... | collective-permute-start | bytes 2359304 | tf_op jit(solution)/shard_map/ppermute | solution.py:379
  38.1 35.4 %collective-permute-start.3 = (bf16[2,256,768]{2,1,0:T(8,128)(2,1)}, bf16[2,256,768]{2,1,0:T(8,128)(2,1)}, u32[]{:S(2)}, u32[]{:S(2)}) collective-permute-start(bf16[2,256,768]{2,1,0:T(8,128)(2,1)} %get-tuple-element.37), channel_id=1, source_target_pairs={{0,4},{1,5},{2,6},{3,7},{4,0},{5,1},{6,2},{7,3},{8,12},{9,13},{10,... | collective-permute-start | bytes 2359304 | tf_op jit(solution)/shard_map/ppermute | solution.py:379
  39.9 34.9 %collective-permute-start.4 = (bf16[2,256,768]{2,1,0:T(8,128)(2,1)}, bf16[2,256,768]{2,1,0:T(8,128)(2,1)}, u32[]{:S(2)}, u32[]{:S(2)}) collective-permute-start(bf16[2,256,768]{2,1,0:T(8,128)(2,1)} %get-tuple-element.38), channel_id=1, source_target_pairs={{0,6},{1,7},{2,0},{3,1},{4,2},{5,3},{6,4},{7,5},{8,14},{9,15},{10,... | collective-permute-start | bytes 2359304 | tf_op jit(solution)/shard_map/ppermute | solution.py:379
  47.3 0.8 copy-start.6
  53.7 21.1 %copy-start.1 = (bf16[8,256,512]{2,1,0:T(8,128)(2,1)S(1)}, bf16[8,256,512]{2,1,0:T(8,128)(2,1)}, u32[]{:S(2)}) copy-start(bf16[8,256,512]{2,1,0:T(8,128)(2,1)} %copy-done) | copy-start | bytes 6291460
  53.7 21.1 %copy-start.3 = (bf16[2,256,768]{2,1,0:T(8,128)(2,1)S(1)}, bf16[2,256,768]{2,1,0:T(8,128)(2,1)}, u32[]{:S(2)}) copy-start(bf16[2,256,768]{2,1,0:T(8,128)(2,1)} %get-tuple-element.35.refs_2_) | copy-start | bytes 2359300
  53.8 21.1 %copy-start.4 = (s32[512]{0:T(512)S(1)}, s32[512]{0:T(512)}, u32[]{:S(2)}) copy-start(s32[512]{0:T(512)} %doc_ref.5) | copy-start | bytes 6148
  53.8 21.1 %copy-start.5 = (s32[16]{0:T(128)S(1)}, s32[16]{0:T(128)}, u32[]{:S(2)}) copy-start(s32[16]{0:T(128)} %select_reduce_fusion.slot_ref) | copy-start | bytes 196
  53.8 21.1 %copy-start.7 = (bf16[896,256]{1,0:T(8,128)(2,1)S(1)}, bf16[896,256]{1,0:T(8,128)(2,1)}, u32[]{:S(2)}) copy-start(bf16[896,256]{1,0:T(8,128)(2,1)} %copy-done.6) | copy-start | bytes 1376260
  53.8 61.4 %all-to-all-start.2 = ((bf16[32,128,256]{2,1,0:T(8,128)(2,1)}), bf16[32,128,256]{2,1,0:T(8,128)(2,1)}, u32[]{:S(2)}, u32[]{:S(2)}) async-start(bf16[32,128,256]{2,1,0:T(8,128)(2,1)} %attend.5), calls=%async_computation.2 | async-start | bytes 4194304 | tf_op jit(solution)/shard_map/all_to_all | solution.py:384
  98.2 2.7 %copy-start.2 = (bf16[32,128,768]{2,1,0:T(8,128)(2,1)}, bf16[32,128,768]{2,1,0:T(8,128)(2,1)S(1)}, u32[]{:S(2)}) copy-start(bf16[32,128,768]{2,1,0:T(8,128)(2,1)S(1)} %attend.3) | copy-start | bytes 18874372
  115.2 147.4 %all-to-all-start.1 = ((bf16[32,128,768]{2,1,0:T(8,128)(2,1)}), bf16[32,128,768]{2,1,0:T(8,128)(2,1)}, u32[]{:S(2)}, u32[]{:S(2)}) async-start(bf16[32,128,768]{2,1,0:T(8,128)(2,1)} %copy-done.2), calls=%async_computation.1 | async-start | bytes 12582912 | tf_op jit(solution)/shard_map/all_to_all | solution.py:384
where the time goes:
time: 267 us
  waiting for transfers between devices  180 us (67%)
  Pallas kernels  50 us (19%)
  starting transfers between devices  30.6 us (11%)
  local copies, waits for them, and re-layouts  4 us (1%)
    all_to_all x2, waiting for transfers between devices, shards(): lax.all_to_all(sent, 'ctx', split_axis=0, concat_axis=0, tiled=True)  152 us
    pallas_call x3, Pallas kernels, attend(): pl.pallas_call(functools.partial(attend_kernel, heads=heads, count=count,...  35.1 us
    all_to_all x2, starting transfers between devices, shards(): lax.all_to_all(sent, 'ctx', split_axis=0, concat_axis=0, tiled=True)  18.9 us
    all_to_all x1, waiting for transfers between devices, shards(): lax.all_to_all(opening, 'head', split_axis=0, concat_axis=0, tiled=True)  16.1 us
    ppermute x3, waiting for transfers between devices, shards(): sources.append(lax.ppermute(part, 'head', onward) if step else part)  8.72 us
    pallas_call x2, Pallas kernels, place(): pl.pallas_call(functools.partial(place_kernel, count=count, first=first,...  6.42 us
  transfers between devices with their start and end apart: 8, of which 7 were waited for; matrix products, arithmetic and copies ran while one was open for 1% of the time, Pallas kernels for 16%

commit v1 on v0

--- a/solution.py
+++ b/solution.py
@@ -18,7 +18,8 @@
 EXP2_SCALE = math.log2(math.e) / math.sqrt(HD)
 
 
-def attend_kernel(doc_ref, slot_ref, order_ref, shard_ref, *refs, heads, count, base, steps, ahead, paired, q_views):
+def attend_kernel(doc_ref, slot_ref, shard_ref, *refs, heads, count, base, steps, ahead, paired, ordered, q_views):
+    order_ref, refs = (refs[0], refs[1:]) if ordered else (None, refs)
     given, (out_ref, win_ref, held_ref, mixed_ref, kv_sems, q_sems, out_sems) = refs[:-7], refs[-7:]
     width = heads * HD
     own_ref = given[0]
@@ -43,7 +44,7 @@
     for view in range(steps):
         which, lead, row, column = q_views[view]
         source = given[which] if lead is None else given[which].at[lead]
-        step = order_ref[view]
+        step = order_ref[view] if ordered else view
         pltpu.make_async_copy(
             source.at[pl.ds(row, BLK), pl.ds(column, width)], held_ref.at[step], q_sems.at[step]
         ).start()
@@ -128,13 +129,14 @@
     given = [own] + ([] if halo is None else [halo])
     views = [(len(given) + which if which >= 0 else 0, lead, row, column) for which, lead, row, column in q_views]
     given = given + list(sources) + ([] if result is None else [result])
+    scalars = [doc_ids, slot, shard] + ([] if order is None else [order])
     smem, anywhere = pl.BlockSpec(memory_space=pltpu.SMEM), pl.BlockSpec(memory_space=pl.ANY)
     return pl.pallas_call(
         functools.partial(
             attend_kernel, heads=heads, count=count, base=base, steps=steps, ahead=ahead, paired=alone,
-            q_views=views
+            ordered=order is not None, q_views=views
         ),
-        in_specs=[smem] * 4 + [anywhere] * len(given),
+        in_specs=[smem] * len(scalars) + [anywhere] * len(given),
         out_specs=pl.BlockSpec(memory_space=pl.ANY),
         out_shape=jax.ShapeDtypeStruct((slots, BLK, width), jnp.bfloat16),
         scratch_shapes=[
@@ -145,13 +147,13 @@
             pltpu.SemaphoreType.DMA((steps,)),
             pltpu.SemaphoreType.DMA((steps,)),
         ],
-        input_output_aliases={} if result is None else {4 + len(given) - 1: 0},
+        input_output_aliases={} if result is None else {len(scalars) + len(given) - 1: 0},
         compiler_params=pltpu.CompilerParams(vmem_limit_bytes=VMEM_BYTES if alone else SHARED_VMEM_BYTES),
         cost_estimate=pl.CostEstimate(
             flops=10**12 if ahead else 0, bytes_accessed=0, transcendentals=0
         ),
         name="attend",
-    )(doc_ids, slot, order, shard, *given)
+    )(*scalars, *given)
 
 
 def first_parts_kernel(k_ref, v_ref, q_ref, out_ref, held_ref, in_sems, out_sems, *, head_count, width):
@@ -367,10 +369,10 @@
         if turn == 0:
             views = [(-1, None, i * BLK, 2 * HD) for i in range(count)]
             sent = attend(
-                opening, None, [], views[MAXDOC:], index, heads, tables, count, shard_count, MAXDOC, count - MAXDOC
+                opening, None, [], views[MAXDOC:], None, heads, tables, count, shard_count, MAXDOC, count - MAXDOC
             )
             sent = attend(
-                opening, halo, [], views[:MAXDOC], index, heads, tables, count, shard_count, 0, MAXDOC, sent
+                opening, halo, [], views[:MAXDOC], None, heads, tables, count, shard_count, 0, MAXDOC, sent
             )
         else:
             sources = []

time: 267 us -> 267 us (level)
  no operation moved by 1% of the time
where the time goes in v1:
time: 267 us
  waiting for transfers between devices  181 us (68%)
  Pallas kernels  50.1 us (19%)
  starting transfers between devices  30.4 us (11%)
  local copies, waits for them, and re-layouts  3.51 us (1%)
    all_to_all x2, waiting for transfers between devices, shards(): lax.all_to_all(sent, 'ctx', split_axis=0, concat_axis=0, tiled=True)  153 us
    pallas_call x3, Pallas kernels, attend(): pl.pallas_call(functools.partial(attend_kernel, heads=heads, count=count,...  35.2 us
    all_to_all x2, starting transfers between devices, shards(): lax.all_to_all(sent, 'ctx', split_axis=0, concat_axis=0, tiled=True)  18.7 us
    all_to_all x1, waiting for transfers between devices, shards(): lax.all_to_all(opening, 'head', split_axis=0, concat_axis=0, tiled=True)  16.1 us
    ppermute x3, waiting for transfers between devices, shards(): sources.append(lax.ppermute(part, 'head', onward) if step else part)  8.59 us
    pallas_call x2, Pallas kernels, place(): pl.pallas_call(functools.partial(place_kernel, count=count, first=first,...  6.42 us
  transfers between devices with their start and end apart: 8, of which 7 were waited for; matrix products, arithmetic and copies ran while one was open for 1% of the time, Pallas kernels for 16%

profile of v1, /device:TPU:33, one launch (start us, length us, event | category | flops | bytes accessed | tf_op | source)
XLA Modules:
  0.0 266.8 jit_solution(15997149725605383766)
XLA Ops:
  0.0 2.6 first_parts.1
  2.6 5.2 %all-to-all-start = ((bf16[8,256,512]{2,1,0:T(8,128)(2,1)}), bf16[8,256,512]{2,1,0:T(8,128)(2,1)S(1)}, u32[]{:S(2)}, u32[]{:S(2)}) async-start(bf16[8,256,512]{2,1,0:T(8,128)(2,1)} %first_parts.1), calls=%async_computation | async-start | bytes 4194304 | tf_op jit(solution)/shard_map/all_to_all | solution.py:345
  7.8 0.6 pad_add_fusion.place_ref
  8.4 0.0 copy-start.8
  8.4 3.6 %later_parts.1 = (bf16[2,256,768]{2,1,0:T(8,128)(2,1)}, bf16[2,256,768]{2,1,0:T(8,128)(2,1)}, bf16[2,256,768]{2,1,0:T(8,128)(2,1)}, bf16[2,256,768]{2,1,0:T(8,128)(2,1)}, bf16[4,256,768]{2,1,0:T(8,128)(2,1)}) custom-call(s32[2]{0:T(128)} %pad_add_fusion.place_ref, bf16[256,8192]{1,0:T(8,128)(2,1)} %q_ref.3), custom_call_target="tpu_custom_call" | custom-call | bytes 8388608 | tf_op jit(solution)/shard_map/later_parts/pallas_call | solution.py:243
  12.0 0.1 collective-permute-start
  12.1 0.0 copy-done.8
  12.1 0.1 and_select_fusion.6
  12.2 0.8 select_reduce_fusion.slot_ref
  13.0 2.9 %collective-permute-done.got_ref = bf16[4,256,768]{2,1,0:T(8,128)(2,1)} collective-permute-done((bf16[4,256,768]{2,1,0:T(8,128)(2,1)}, bf16[4,256,768]{2,1,0:T(8,128)(2,1)}, u32[]{:S(2)}, u32[]{:S(2)}) %collective-permute-start) | collective-permute-done | bytes 1572896 | tf_op jit(solution)/shard_map/ppermute | solution.py:344
  15.8 2.2 fill.1
  18.1 16.1 %all-to-all-done = bf16[8,256,512]{2,1,0:T(8,128)(2,1)S(1)} async-done(((bf16[8,256,512]{2,1,0:T(8,128)(2,1)}), bf16[8,256,512]{2,1,0:T(8,128)(2,1)S(1)}, u32[]{:S(2)}, u32[]{:S(2)}) %all-to-all-start) | async-done | bytes 2097184 | tf_op jit(solution)/shard_map/all_to_all | solution.py:345
  34.1 0.0 copy-start
  34.2 3.5 %collective-permute-start.1 = (bf16[896,256]{1,0:T(8,128)(2,1)S(1)}, bf16[896,256]{1,0:T(8,128)(2,1)S(1)}, u32[]{:S(2)}, u32[]{:S(2)}) collective-permute-start(bf16[896,256]{1,0:T(8,128)(2,1)S(1)} %slice.4), channel_id=1, source_target_pairs={{0,8},{8,16},{16,24},{24,32},{32,40},{40,48},{48,56},{56,64},{64,7... | collective-permute-start | bytes 1376264 | tf_op jit(solution)/shard_map/ppermute | solution.py:362
  37.7 0.4 collective-permute-start.2
  38.1 1.8 collective-permute-start.3
  39.9 0.7 collective-permute-start.4
  40.6 0.0 copy-done
  40.6 5.9 %attend.4.refs_2_ = bf16[32,128,256]{2,1,0:T(8,128)(2,1)} custom-call(s32[512]{0:T(512)} %doc_ref.5, s32[16]{0:T(128)} %select_reduce_fusion.slot_ref, s32[1]{0:T(128)} %bitcast.2.shard_ref, bf16[2048,512]{1,0:T(8,128)(2,1)} %bitcast.5), custom_call_target="tpu_custom_call" | custom-call | tf_op jit(solution)/shard_map/attend/pallas_call | solution.py:134
  46.5 0.9 collective-permute-done.1.refs_2_.refs_1_
  47.3 0.0 copy-start.6
  47.3 0.8 copy-done.6
  48.1 5.9 %attend.5 = bf16[32,128,256]{2,1,0:T(8,128)(2,1)} custom-call(s32[512]{0:T(512)} %doc_ref.5, s32[16]{0:T(128)} %select_reduce_fusion.slot_ref, s32[1]{0:T(128)} %bitcast.2.shard_ref, bf16[2048,512]{1,0:T(8,128)(2,1)} %bitcast.6, bf16[896,256]{1,0:T(8,128)(2,1)} %copy-done.6, bf16[32,128,256]{2,1,0:T(8,128)(2,1)} %attend.4.refs_2_), custom_call_target="tpu_custom_call", output_to_operand_aliasing={{}: (5, {})} | custom-call | flops 999999995904 | tf_op jit(solution)/shard_map/attend/pallas_call | solution.py:134
  54.1 0.0 copy-start.1
  54.1 0.0 copy-start.3
  54.1 0.0 copy-start.4
  54.1 0.0 copy-start.5
  54.1 0.0 copy-start.7
  54.1 12.1 %all-to-all-start.2 = ((bf16[32,128,256]{2,1,0:T(8,128)(2,1)}), bf16[32,128,256]{2,1,0:T(8,128)(2,1)}, u32[]{:S(2)}, u32[]{:S(2)}) async-start(bf16[32,128,256]{2,1,0:T(8,128)(2,1)} %attend.5), calls=%async_computation.2 | async-start | bytes 4194304 | tf_op jit(solution)/shard_map/all_to_all | solution.py:386
  66.2 0.0 collective-permute-done.2.refs_4_
  66.2 7.3 %collective-permute-done.3.refs_5_ = bf16[2,256,768]{2,1,0:T(8,128)(2,1)} collective-permute-done((bf16[2,256,768]{2,1,0:T(8,128)(2,1)}, bf16[2,256,768]{2,1,0:T(8,128)(2,1)}, u32[]{:S(2)}, u32[]{:S(2)}) %collective-permute-start.3) | collective-permute-done | bytes 786464 | tf_op jit(solution)/shard_map/ppermute | solution.py:381
  73.5 1.3 collective-permute-done.4.refs_6_
  74.8 0.0 copy-done.1
  74.8 0.0 copy-done.3
  74.8 0.0 copy-done.4
  74.8 0.0 copy-done.5
  74.8 0.0 copy-done.7
  74.8 23.4 %attend.3 = bf16[32,128,768]{2,1,0:T(8,128)(2,1)S(1)} custom-call(s32[512]{0:T(512)S(1)} %copy-done.4, s32[16]{0:T(128)S(1)} %copy-done.5, s32[1]{0:T(128)} %bitcast.2.shard_ref, s32[16]{0:T(128)S(1)} %get-tuple-element.33.refs_0_, bf16[2048,512]{1,0:T(8,128)(2,1)S(1)} %bitcast.7, bf16[896,256]{1,0:T(8,128)(2,1)S(1)} %copy-done.7, ...), custom_call_target="tpu_custom_call" | custom-call | flops 999999995904 | tf_op jit(solution)/shard_map/attend/pallas_call | solution.py:134
  98.3 0.0 copy-start.2
  98.3 2.7 copy-done.2
  100.9 14.4 %all-to-all-done.2.refs_0_ = bf16[32,128,256]{2,1,0:T(8,128)(2,1)} async-done(((bf16[32,128,256]{2,1,0:T(8,128)(2,1)}), bf16[32,128,256]{2,1,0:T(8,128)(2,1)}, u32[]{:S(2)}, u32[]{:S(2)}) %all-to-all-start.2) | async-done | bytes 2097184 | tf_op jit(solution)/shard_map/all_to_all | solution.py:386
  115.4 6.6 %all-to-all-start.1 = ((bf16[32,128,768]{2,1,0:T(8,128)(2,1)}), bf16[32,128,768]{2,1,0:T(8,128)(2,1)}, u32[]{:S(2)}, u32[]{:S(2)}) async-start(bf16[32,128,768]{2,1,0:T(8,128)(2,1)} %copy-done.2), calls=%async_computation.1 | async-start | bytes 12582912 | tf_op jit(solution)/shard_map/all_to_all | solution.py:386
  122.0 2.7 %place.2.refs_1_ = bf16[2048,1024]{1,0:T(8,128)(2,1)} custom-call(s32[16]{0:T(128)S(1)} %get-tuple-element.31.source_ref, bf16[32,128,256]{2,1,0:T(8,128)(2,1)} %all-to-all-done.2.refs_0_), custom_call_target="tpu_custom_call" | custom-call | bytes 2097152 | tf_op jit(solution)/shard_map/place/pallas_call | solution.py:310
  124.7 138.2 %all-to-all-done.1.refs_0_ = bf16[32,128,768]{2,1,0:T(8,128)(2,1)} async-done(((bf16[32,128,768]{2,1,0:T(8,128)(2,1)}), bf16[32,128,768]{2,1,0:T(8,128)(2,1)}, u32[]{:S(2)}, u32[]{:S(2)}) %all-to-all-start.1) | async-done | bytes 6291488 | tf_op jit(solution)/shard_map/all_to_all | solution.py:386
  262.9 3.7 %place.3 = bf16[2048,1024]{1,0:T(8,128)(2,1)} custom-call(s32[16]{0:T(128)S(1)} %get-tuple-element.31.source_ref, bf16[32,128,768]{2,1,0:T(8,128)(2,1)} %all-to-all-done.1.refs_0_, bf16[2048,1024]{1,0:T(8,128)(2,1)} %place.2.refs_1_), custom_call_target="tpu_custom_call", output_to_operand_aliasing={{}: (2, {})} | custom-call | bytes 6291456 | tf_op jit(solution)/shard_map/place/pallas_call | solution.py:310
  (3 shorter events, 0.0 us)
Async XLA Ops:
  2.6 31.5 %all-to-all-start = ((bf16[8,256,512]{2,1,0:T(8,128)(2,1)}), bf16[8,256,512]{2,1,0:T(8,128)(2,1)S(1)}, u32[]{:S(2)}, u32[]{:S(2)}) async-start(bf16[8,256,512]{2,1,0:T(8,128)(2,1)} %first_parts.1), calls=%async_computation | async-start | bytes 4194304 | tf_op jit(solution)/shard_map/all_to_all | solution.py:345
  8.4 3.7 %copy-start.8 = (s32[512]{0:T(512)S(1)}, s32[512]{0:T(512)}, u32[]{:S(2)}) copy-start(s32[512]{0:T(512)} %param.9) | copy-start | bytes 6148
  12.0 3.8 %collective-permute-start = (bf16[4,256,768]{2,1,0:T(8,128)(2,1)}, bf16[4,256,768]{2,1,0:T(8,128)(2,1)}, u32[]{:S(2)}, u32[]{:S(2)}) collective-permute-start(bf16[4,256,768]{2,1,0:T(8,128)(2,1)} %get-tuple-element.22), channel_id=1, source_target_pairs={{0,1},{1,0},{2,3},{3,2},{4,5},{5,4},{6,7},{7,6},{8,9},{9,8},{10,11... | collective-permute-start | bytes 4718600 | tf_op jit(solution)/shard_map/ppermute | solution.py:344
  34.1 6.4 %copy-start = (bf16[8,256,512]{2,1,0:T(8,128)(2,1)}, bf16[8,256,512]{2,1,0:T(8,128)(2,1)S(1)}, u32[]{:S(2)}) copy-start(bf16[8,256,512]{2,1,0:T(8,128)(2,1)S(1)} %all-to-all-done) | copy-start | bytes 6291460
  34.2 13.2 %collective-permute-start.1 = (bf16[896,256]{1,0:T(8,128)(2,1)S(1)}, bf16[896,256]{1,0:T(8,128)(2,1)S(1)}, u32[]{:S(2)}, u32[]{:S(2)}) collective-permute-start(bf16[896,256]{1,0:T(8,128)(2,1)S(1)} %slice.4), channel_id=1, source_target_pairs={{0,8},{8,16},{16,24},{24,32},{32,40},{40,48},{48,56},{56,64},{64,7... | collective-permute-start | bytes 1376264 | tf_op jit(solution)/shard_map/ppermute | solution.py:362
  37.7 28.5 %collective-permute-start.2 = (bf16[2,256,768]{2,1,0:T(8,128)(2,1)}, bf16[2,256,768]{2,1,0:T(8,128)(2,1)}, u32[]{:S(2)}, u32[]{:S(2)}) collective-permute-start(bf16[2,256,768]{2,1,0:T(8,128)(2,1)} %get-tuple-element.36), channel_id=1, source_target_pairs={{0,2},{1,3},{2,4},{3,5},{4,6},{5,7},{6,0},{7,1},{8,10},{9,11},{10,... | collective-permute-start | bytes 2359304 | tf_op jit(solution)/shard_map/ppermute | solution.py:381
  38.1 35.4 %collective-permute-start.3 = (bf16[2,256,768]{2,1,0:T(8,128)(2,1)}, bf16[2,256,768]{2,1,0:T(8,128)(2,1)}, u32[]{:S(2)}, u32[]{:S(2)}) collective-permute-start(bf16[2,256,768]{2,1,0:T(8,128)(2,1)} %get-tuple-element.37), channel_id=1, source_target_pairs={{0,4},{1,5},{2,6},{3,7},{4,0},{5,1},{6,2},{7,3},{8,12},{9,13},{10,... | collective-permute-start | bytes 2359304 | tf_op jit(solution)/shard_map/ppermute | solution.py:381
  39.9 34.9 %collective-permute-start.4 = (bf16[2,256,768]{2,1,0:T(8,128)(2,1)}, bf16[2,256,768]{2,1,0:T(8,128)(2,1)}, u32[]{:S(2)}, u32[]{:S(2)}) collective-permute-start(bf16[2,256,768]{2,1,0:T(8,128)(2,1)} %get-tuple-element.38), channel_id=1, source_target_pairs={{0,6},{1,7},{2,0},{3,1},{4,2},{5,3},{6,4},{7,5},{8,14},{9,15},{10,... | collective-permute-start | bytes 2359304 | tf_op jit(solution)/shard_map/ppermute | solution.py:381
  47.3 0.8 copy-start.6
  54.1 20.8 %copy-start.1 = (bf16[8,256,512]{2,1,0:T(8,128)(2,1)S(1)}, bf16[8,256,512]{2,1,0:T(8,128)(2,1)}, u32[]{:S(2)}) copy-start(bf16[8,256,512]{2,1,0:T(8,128)(2,1)} %copy-done) | copy-start | bytes 6291460
  54.1 20.7 %copy-start.3 = (bf16[2,256,768]{2,1,0:T(8,128)(2,1)S(1)}, bf16[2,256,768]{2,1,0:T(8,128)(2,1)}, u32[]{:S(2)}) copy-start(bf16[2,256,768]{2,1,0:T(8,128)(2,1)} %get-tuple-element.35.refs_3_) | copy-start | bytes 2359300
  54.1 20.7 %copy-start.4 = (s32[512]{0:T(512)S(1)}, s32[512]{0:T(512)}, u32[]{:S(2)}) copy-start(s32[512]{0:T(512)} %doc_ref.5) | copy-start | bytes 6148
  54.1 20.7 %copy-start.5 = (s32[16]{0:T(128)S(1)}, s32[16]{0:T(128)}, u32[]{:S(2)}) copy-start(s32[16]{0:T(128)} %select_reduce_fusion.slot_ref) | copy-start | bytes 196
  54.1 20.7 %copy-start.7 = (bf16[896,256]{1,0:T(8,128)(2,1)S(1)}, bf16[896,256]{1,0:T(8,128)(2,1)}, u32[]{:S(2)}) copy-start(bf16[896,256]{1,0:T(8,128)(2,1)} %copy-done.6) | copy-start | bytes 1376260
  54.1 61.2 %all-to-all-start.2 = ((bf16[32,128,256]{2,1,0:T(8,128)(2,1)}), bf16[32,128,256]{2,1,0:T(8,128)(2,1)}, u32[]{:S(2)}, u32[]{:S(2)}) async-start(bf16[32,128,256]{2,1,0:T(8,128)(2,1)} %attend.5), calls=%async_computation.2 | async-start | bytes 4194304 | tf_op jit(solution)/shard_map/all_to_all | solution.py:386
  98.3 2.7 copy-start.2
  115.4 147.5 %all-to-all-start.1 = ((bf16[32,128,768]{2,1,0:T(8,128)(2,1)}), bf16[32,128,768]{2,1,0:T(8,128)(2,1)}, u32[]{:S(2)}, u32[]{:S(2)}) async-start(bf16[32,128,768]{2,1,0:T(8,128)(2,1)} %copy-done.2), calls=%async_computation.1 | async-start | bytes 12582912 | tf_op jit(solution)/shard_map/all_to_all | solution.py:386

commit v2 on v1

--- a/solution.py
+++ b/solution.py
@@ -14,7 +14,7 @@
 VMEM_BYTES = 60 * 1024 * 1024
 SHARED_VMEM_BYTES = 32 * 1024 * 1024
 HALO = MAXDOC - 1
-CHUNKS = (2, 6)
+CHUNKS = (1, 3, 4)
 EXP2_SCALE = math.log2(math.e) / math.sqrt(HD)
 
 
@@ -375,8 +375,11 @@
                 opening, halo, [], views[:MAXDOC], None, heads, tables, count, shard_count, 0, MAXDOC, sent
             )
         else:
+            parts = later[turn - 1]
+            if turn > 1:
+                parts, _ = lax.optimization_barrier((parts, sent))
             sources = []
-            for step, part in enumerate(later[turn - 1]):
+            for step, part in enumerate(parts):
                 onward = [(h, (h + 2 * step) % head_count) for h in range(head_count)]
                 sources.append(lax.ppermute(part, "head", onward) if step else part)
             views = [

time: 267 us -> 272 us (1.019)
  waiting for transfers between devices: 181 us -> 151 us
  Pallas kernels: 50.1 us -> 67.7 us
  starting transfers between devices: 30.4 us -> 42.5 us
  local copies, waits for them, and re-layouts: 3.51 us -> 8.4 us
    all_to_all x2 -> x3, waiting for transfers between devices: 153 us -> 128 us  [shards(): lax.all_to_all(sent, 'ctx', split_axis=0, concat_axis=0, tiled=True)]
    pallas_call x3 -> x4, Pallas kernels: 35.2 us -> 48.3 us  [attend(): pl.pallas_call(functools.partial(attend_kernel, heads=heads, count=count,...]
    all_to_all x1, waiting for transfers between devices: 16.1 us -> 5.52 us  [shards(): lax.all_to_all(opening, 'head', split_axis=0, concat_axis=0, tiled=True)]
    all_to_all x2 -> x3, starting transfers between devices: 18.7 us -> 26.6 us  [shards(): lax.all_to_all(sent, 'ctx', split_axis=0, concat_axis=0, tiled=True)]
    unnamed x18 -> x28, local copies, waits for them, and re-layouts: 3.48 us -> 8.37 us
    ppermute x3 -> x6, waiting for transfers between devices: 8.59 us -> 12.6 us  [shards(): sources.append(lax.ppermute(part, 'head', onward) if step else part)]
    ppermute x3 -> x6, starting transfers between devices: 2.86 us -> 6.61 us  [shards(): sources.append(lax.ppermute(part, 'head', onward) if step else part)]
    pallas_call x2 -> x3, Pallas kernels: 6.42 us -> 8.5 us  [place(): pl.pallas_call(functools.partial(place_kernel, count=count, first=first,...]
  transfers between devices with their start and end apart: 8 -> 13, of which waited for: 7 -> 8; matrix products, arithmetic and copies ran while one was open for 1% -> 1% of each run, Pallas kernels for 16% -> 23%
where the time goes in v2:
time: 272 us; the launch traced here: 271 us
  waiting for transfers between devices  151 us (56%)
  Pallas kernels  67.7 us (25%)
  starting transfers between devices  42.5 us (16%)
  local copies, waits for them, and re-layouts  8.4 us (3%)
    all_to_all x3, waiting for transfers between devices, shards(): lax.all_to_all(sent, 'ctx', split_axis=0, concat_axis=0, tiled=True)  128 us
    pallas_call x4, Pallas kernels, attend(): pl.pallas_call(functools.partial(attend_kernel, heads=heads, count=count,...  48.3 us
    all_to_all x3, starting transfers between devices, shards(): lax.all_to_all(sent, 'ctx', split_axis=0, concat_axis=0, tiled=True)  26.6 us
    ppermute x6, waiting for transfers between devices, shards(): sources.append(lax.ppermute(part, 'head', onward) if step else part)  12.6 us
    pallas_call x3, Pallas kernels, place(): pl.pallas_call(functools.partial(place_kernel, count=count, first=first,...  8.5 us
    unnamed x28, local copies, waits for them, and re-layouts  8.37 us
    ppermute x6, starting transfers between devices, shards(): sources.append(lax.ppermute(part, 'head', onward) if step else part)  6.61 us
    all_to_all x1, waiting for transfers between devices, shards(): lax.all_to_all(opening, 'head', split_axis=0, concat_axis=0, tiled=True)  5.52 us
  transfers between devices with their start and end apart: 13, of which 8 were waited for; matrix products, arithmetic and copies ran while one was open for 1% of the time, Pallas kernels for 23%

profile of v2, /device:TPU:33, one launch (start us, length us, event | category | flops | bytes accessed | tf_op | source)
XLA Modules:
  0.0 271.1 jit_solution(11066398588737243160)
XLA Ops:
  0.0 2.4 first_parts.1
  2.4 0.0 copy-start.13
  2.4 5.2 %all-to-all-start = ((bf16[8,256,384]{2,1,0:T(8,128)(2,1)}), bf16[8,256,384]{2,1,0:T(8,128)(2,1)S(1)}, u32[]{:S(2)}, u32[]{:S(2)}) async-start(bf16[8,256,384]{2,1,0:T(8,128)(2,1)} %first_parts.1), calls=%async_computation | async-start | bytes 3145728 | tf_op jit(solution)/shard_map/all_to_all | solution.py:345
  7.6 0.7 pad_add_fusion.place_ref
  8.2 4.5 %later_parts.1 = (bf16[2,256,384]{2,1,0:T(8,128)(2,1)}, bf16[2,256,384]{2,1,0:T(8,128)(2,1)}, bf16[2,256,384]{2,1,0:T(8,128)(2,1)}, bf16[2,256,384]{2,1,0:T(8,12...) custom-call(s32[2]{0:T(128)} %pad_add_fusion.place_ref, ...), custom_call_target="tpu_custom_call" | custom-call | bytes 8388608 | tf_op jit(solution)/shard_map/later_parts/pallas_call | solution.py:243
  12.8 0.1 collective-permute-start.1
  12.9 0.5 collective-permute-start
  13.4 0.1 and_select_fusion.6
  13.5 0.8 select_reduce_fusion.slot_ref
  14.2 2.6 collective-permute-done.got_ref
  16.9 0.9 copy-done.12
  17.8 2.0 fill.2
  19.7 0.0 collective-permute-done.1.got_ref
  19.8 1.0 copy-done.11
  20.7 2.0 fill.3
  22.8 5.5 %all-to-all-done = bf16[8,256,384]{2,1,0:T(8,128)(2,1)S(1)} async-done(((bf16[8,256,384]{2,1,0:T(8,128)(2,1)}), bf16[8,256,384]{2,1,0:T(8,128)(2,1)S(1)}, u32[]{:S(2)}, u32[]{:S(2)}) %all-to-all-start) | async-done | bytes 1572896 | tf_op jit(solution)/shard_map/all_to_all | solution.py:345
  28.3 3.5 %collective-permute-start.2 = (bf16[896,256]{1,0:T(8,128)(2,1)S(1)}, bf16[896,256]{1,0:T(8,128)(2,1)S(1)}, u32[]{:S(2)}, u32[]{:S(2)}) collective-permute-start(bf16[896,256]{1,0:T(8,128)(2,1)S(1)} %slice.4), channel_id=1, source_target_pairs={{0,8},{8,16},{16,24},{24,32},{32,40},{40,48},{48,56},{56,64},{64,7... | collective-permute-start | bytes 1376264 | tf_op jit(solution)/shard_map/ppermute | solution.py:362
  31.9 0.4 collective-permute-start.3
  32.2 1.8 collective-permute-start.4
  34.0 0.7 collective-permute-start.5
  34.7 5.3 %attend.6.refs_2_ = bf16[32,128,128]{2,1,0:T(8,128)(2,1)} custom-call(s32[512]{0:T(512)} %doc_ref.7, s32[16]{0:T(128)} %select_reduce_fusion.slot_ref, s32[1]{0:T(128)} %bitcast.2.shard_ref, bf16[2048,384]{1,0:T(8,128)(2,1)} %bitcast.5), custom_call_target="tpu_custom_call" | custom-call | tf_op jit(solution)/shard_map/attend/pallas_call | solution.py:134
  40.0 1.4 collective-permute-done.2.refs_2_.refs_1_
  41.5 0.8 copy-done.8
  42.3 5.4 %attend.7 = bf16[32,128,128]{2,1,0:T(8,128)(2,1)} custom-call(s32[512]{0:T(512)} %doc_ref.7, s32[16]{0:T(128)} %select_reduce_fusion.slot_ref, s32[1]{0:T(128)} %bitcast.2.shard_ref, bf16[2048,384]{1,0:T(8,128)(2,1)} %bitcast.6, bf16[896,256]{1,0:T(8,128)(2,1)} %copy-done.8, bf16[32,128,128]{2,1,0:T(8,128)(2,1)} %attend.6.refs_2_), custom_call_target="tpu_custom_call", output_to_operand_aliasing={{}: (5, {})} | custom-call | flops 999999995904 | tf_op jit(solution)/shard_map/attend/pallas_call | solution.py:134
  47.7 11.9 %all-to-all-start.3 = ((bf16[32,128,128]{2,1,0:T(8,128)(2,1)}), bf16[32,128,128]{2,1,0:T(8,128)(2,1)}, u32[]{:S(2)}, u32[]{:S(2)}) async-start(bf16[32,128,128]{2,1,0:T(8,128)(2,1)} %attend.7), calls=%async_computation.3 | async-start | bytes 2097152 | tf_op jit(solution)/shard_map/all_to_all | solution.py:389
  59.6 0.0 collective-permute-done.3.refs_4_
  59.6 0.0 collective-permute-done.4.refs_5_
  59.7 1.0 copy-done.9
  60.7 16.6 %attend.4 = bf16[32,128,384]{2,1,0:T(8,128)(2,1)S(1)} custom-call(s32[512]{0:T(512)S(1)} %copy-done.6, s32[16]{0:T(128)S(1)} %copy-done.7, s32[1]{0:T(128)} %bitcast.2.shard_ref, s32[16]{0:T(128)S(1)} %get-tuple-element.59.refs_0_, bf16[2048,384]{1,0:T(8,128)(2,1)S(1)} %bitcast.7, bf16[896,256]{1,0:T(8,128)(2,1)S(1)} %copy-done.9, ...), custom_call_target="tpu_custom_call" | custom-call | flops 999999995904 | tf_op jit(solution)/shard_map/attend/pallas_call | solution.py:134
  77.3 0.0 copy-start.3
  77.3 1.7 copy-done.3
  79.0 1.1 collective-permute-start.6
  80.1 2.2 collective-permute-start.7
  82.3 0.5 collective-permute-start.8
  82.7 2.9 %all-to-all-done.3.refs_0_ = bf16[32,128,128]{2,1,0:T(8,128)(2,1)} async-done(((bf16[32,128,128]{2,1,0:T(8,128)(2,1)}), bf16[32,128,128]{2,1,0:T(8,128)(2,1)}, u32[]{:S(2)}, u32[]{:S(2)}) %all-to-all-start.3) | async-done | bytes 1048608 | tf_op jit(solution)/shard_map/all_to_all | solution.py:389
  85.6 6.9 %all-to-all-start.2 = ((bf16[32,128,384]{2,1,0:T(8,128)(2,1)}), bf16[32,128,384]{2,1,0:T(8,128)(2,1)}, u32[]{:S(2)}, u32[]{:S(2)}) async-start(bf16[32,128,384]{2,1,0:T(8,128)(2,1)} %copy-done.3), calls=%async_computation.2 | async-start | bytes 6291456 | tf_op jit(solution)/shard_map/all_to_all | solution.py:389
  92.6 0.0 collective-permute-done.6.refs_4_
  92.6 11.0 %collective-permute-done.7.refs_5_ = bf16[2,256,512]{2,1,0:T(8,128)(2,1)S(1)} collective-permute-done((bf16[2,256,512]{2,1,0:T(8,128)(2,1)}, bf16[2,256,512]{2,1,0:T(8,128)(2,1)S(1)}, u32[]{:S(2)}, u32[]{:S(2)}) %collective-permute-start.7) | collective-permute-done | bytes 524320 | tf_op jit(solution)/shard_map/ppermute | solution.py:384
  103.6 1.6 collective-permute-done.8.refs_6_
  105.2 1.0 copy-done.10
  106.2 21.0 %attend.5 = bf16[32,128,512]{2,1,0:T(8,128)(2,1)S(1)} custom-call(s32[512]{0:T(512)S(1)} %copy-done.6, s32[16]{0:T(128)S(1)} %copy-done.7, s32[1]{0:T(128)} %bitcast.2.shard_ref, s32[16]{0:T(128)S(1)} %get-tuple-element.59.refs_0_, bf16[2048,384]{1,0:T(8,128)(2,1)S(1)} %bitcast.8, bf16[896,256]{1,0:T(8,128)(2,1)S(1)} %copy-done.10, ...), custom_call_target="tpu_custom_call" | custom-call | flops 999999995904 | tf_op jit(solution)/shard_map/attend/pallas_call | solution.py:134
  127.2 2.0 copy-done.2
  129.2 34.6 %all-to-all-done.2.refs_0_ = bf16[32,128,384]{2,1,0:T(8,128)(2,1)} async-done(((bf16[32,128,384]{2,1,0:T(8,128)(2,1)}), bf16[32,128,384]{2,1,0:T(8,128)(2,1)}, u32[]{:S(2)}, u32[]{:S(2)}) %all-to-all-start.2) | async-done | bytes 3145760 | tf_op jit(solution)/shard_map/all_to_all | solution.py:389
  163.8 7.7 %all-to-all-start.1 = ((bf16[32,128,512]{2,1,0:T(8,128)(2,1)}), bf16[32,128,512]{2,1,0:T(8,128)(2,1)}, u32[]{:S(2)}, u32[]{:S(2)}) async-start(bf16[32,128,512]{2,1,0:T(8,128)(2,1)} %copy-done.2), calls=%async_computation.1 | async-start | bytes 8388608 | tf_op jit(solution)/shard_map/all_to_all | solution.py:389
  171.5 2.4 place.3.refs_1_
  174.0 2.9 %place.4.refs_1_ = bf16[2048,1024]{1,0:T(8,128)(2,1)} custom-call(s32[16]{0:T(128)S(1)} %get-tuple-element.57.source_ref, bf16[32,128,384]{2,1,0:T(8,128)(2,1)} %all-to-all-done.2.refs_0_, bf16[2048,1024]{1,0:T(8,128)(2,1)} %place.3.refs_1_), custom_call_target="tpu_custom_call", output_to_operand_aliasing={{}: (2, {})} | custom-call | bytes 3145728 | tf_op jit(solution)/shard_map/place/pallas_call | solution.py:310
  176.9 90.9 %all-to-all-done.1.refs_0_ = bf16[32,128,512]{2,1,0:T(8,128)(2,1)} async-done(((bf16[32,128,512]{2,1,0:T(8,128)(2,1)}), bf16[32,128,512]{2,1,0:T(8,128)(2,1)}, u32[]{:S(2)}, u32[]{:S(2)}) %all-to-all-start.1) | async-done | bytes 4194336 | tf_op jit(solution)/shard_map/all_to_all | solution.py:389
  267.8 3.1 %place.5 = bf16[2048,1024]{1,0:T(8,128)(2,1)} custom-call(s32[16]{0:T(128)S(1)} %get-tuple-element.57.source_ref, bf16[32,128,512]{2,1,0:T(8,128)(2,1)} %all-to-all-done.1.refs_0_, bf16[2048,1024]{1,0:T(8,128)(2,1)} %place.4.refs_1_), custom_call_target="tpu_custom_call", output_to_operand_aliasing={{}: (2, {})} | custom-call | bytes 4194304 | tf_op jit(solution)/shard_map/place/pallas_call | solution.py:310
  (23 shorter events, 0.1 us)
Async XLA Ops:
  2.4 11.0 %copy-start.13 = (s32[512]{0:T(512)S(1)}, s32[512]{0:T(512)}, u32[]{:S(2)}) copy-start(s32[512]{0:T(512)} %param.9) | copy-start | bytes 6148
  2.4 25.9 %all-to-all-start = ((bf16[8,256,384]{2,1,0:T(8,128)(2,1)}), bf16[8,256,384]{2,1,0:T(8,128)(2,1)S(1)}, u32[]{:S(2)}, u32[]{:S(2)}) async-start(bf16[8,256,384]{2,1,0:T(8,128)(2,1)} %first_parts.1), calls=%async_computation | async-start | bytes 3145728 | tf_op jit(solution)/shard_map/all_to_all | solution.py:345
  12.8 7.0 %collective-permute-start.1 = (bf16[4,256,512]{2,1,0:T(8,128)(2,1)}, bf16[4,256,512]{2,1,0:T(8,128)(2,1)S(1)}, u32[]{:S(2)}, u32[]{:S(2)}) collective-permute-start(bf16[4,256,512]{2,1,0:T(8,128)(2,1)} %get-tuple-element.48), channel_id=1, source_target_pairs={{0,1},{1,0},{2,3},{3,2},{4,5},{5,4},{6,7},{7,6},{8,9},{9,8},{10,11... | collective-permute-start | bytes 3145736 | tf_op jit(solution)/shard_map/ppermute | solution.py:344
  12.9 4.0 %collective-permute-start = (bf16[4,256,384]{2,1,0:T(8,128)(2,1)}, bf16[4,256,384]{2,1,0:T(8,128)(2,1)S(1)}, u32[]{:S(2)}, u32[]{:S(2)}) collective-permute-start(bf16[4,256,384]{2,1,0:T(8,128)(2,1)} %get-tuple-element.39), channel_id=1, source_target_pairs={{0,1},{1,0},{2,3},{3,2},{4,5},{5,4},{6,7},{7,6},{8,9},{9,8},{10,11... | collective-permute-start | bytes 2359304 | tf_op jit(solution)/shard_map/ppermute | solution.py:344
  16.9 0.9 copy-start.12
  19.8 1.0 copy-start.11
  28.3 6.5 %copy-start = (bf16[8,256,384]{2,1,0:T(8,128)(2,1)}, bf16[8,256,384]{2,1,0:T(8,128)(2,1)S(1)}, u32[]{:S(2)}) copy-start(bf16[8,256,384]{2,1,0:T(8,128)(2,1)S(1)} %all-to-all-done) | copy-start | bytes 4718596
  28.3 13.2 %collective-permute-start.2 = (bf16[896,256]{1,0:T(8,128)(2,1)S(1)}, bf16[896,256]{1,0:T(8,128)(2,1)S(1)}, u32[]{:S(2)}, u32[]{:S(2)}) collective-permute-start(bf16[896,256]{1,0:T(8,128)(2,1)S(1)} %slice.4), channel_id=1, source_target_pairs={{0,8},{8,16},{16,24},{24,32},{32,40},{40,48},{48,56},{56,64},{64,7... | collective-permute-start | bytes 1376264 | tf_op jit(solution)/shard_map/ppermute | solution.py:362
  31.9 27.7 %collective-permute-start.3 = (bf16[2,256,384]{2,1,0:T(8,128)(2,1)}, bf16[2,256,384]{2,1,0:T(8,128)(2,1)}, u32[]{:S(2)}, u32[]{:S(2)}) collective-permute-start(bf16[2,256,384]{2,1,0:T(8,128)(2,1)} %get-tuple-element.66), channel_id=1, source_target_pairs={{0,2},{1,3},{2,4},{3,5},{4,6},{5,7},{6,0},{7,1},{8,10},{9,11},{10,... | collective-permute-start | bytes 1179656 | tf_op jit(solution)/shard_map/ppermute | solution.py:384
  32.2 27.4 %collective-permute-start.4 = (bf16[2,256,384]{2,1,0:T(8,128)(2,1)}, bf16[2,256,384]{2,1,0:T(8,128)(2,1)}, u32[]{:S(2)}, u32[]{:S(2)}) collective-permute-start(bf16[2,256,384]{2,1,0:T(8,128)(2,1)} %get-tuple-element.67), channel_id=1, source_target_pairs={{0,4},{1,5},{2,6},{3,7},{4,0},{5,1},{6,2},{7,3},{8,12},{9,13},{10,... | collective-permute-start | bytes 1179656 | tf_op jit(solution)/shard_map/ppermute | solution.py:384
  34.0 25.6 %collective-permute-start.5 = (bf16[2,256,384]{2,1,0:T(8,128)(2,1)}, bf16[2,256,384]{2,1,0:T(8,128)(2,1)}, u32[]{:S(2)}, u32[]{:S(2)}) collective-permute-start(bf16[2,256,384]{2,1,0:T(8,128)(2,1)} %get-tuple-element.68), channel_id=1, source_target_pairs={{0,6},{1,7},{2,0},{3,1},{4,2},{5,3},{6,4},{7,5},{8,14},{9,15},{10,... | collective-permute-start | bytes 1179656 | tf_op jit(solution)/shard_map/ppermute | solution.py:384
  41.5 0.8 copy-start.8
  42.3 17.4 %copy-start.1 = (bf16[8,256,384]{2,1,0:T(8,128)(2,1)S(1)}, bf16[8,256,384]{2,1,0:T(8,128)(2,1)}, u32[]{:S(2)}) copy-start(bf16[8,256,384]{2,1,0:T(8,128)(2,1)} %copy-done) | copy-start | bytes 4718596
  42.3 17.4 %copy-start.5 = (bf16[2,256,384]{2,1,0:T(8,128)(2,1)S(1)}, bf16[2,256,384]{2,1,0:T(8,128)(2,1)}, u32[]{:S(2)}) copy-start(bf16[2,256,384]{2,1,0:T(8,128)(2,1)} %get-tuple-element.65.refs_3_) | copy-start | bytes 1179652
  42.3 17.4 %copy-start.6 = (s32[512]{0:T(512)S(1)}, s32[512]{0:T(512)}, u32[]{:S(2)}) copy-start(s32[512]{0:T(512)} %doc_ref.7) | copy-start | bytes 6148
  42.3 17.4 %copy-start.7 = (s32[16]{0:T(128)S(1)}, s32[16]{0:T(128)}, u32[]{:S(2)}) copy-start(s32[16]{0:T(128)} %select_reduce_fusion.slot_ref) | copy-start | bytes 196
  47.7 38.0 %all-to-all-start.3 = ((bf16[32,128,128]{2,1,0:T(8,128)(2,1)}), bf16[32,128,128]{2,1,0:T(8,128)(2,1)}, u32[]{:S(2)}, u32[]{:S(2)}) async-start(bf16[32,128,128]{2,1,0:T(8,128)(2,1)} %attend.7), calls=%async_computation.3 | async-start | bytes 2097152 | tf_op jit(solution)/shard_map/all_to_all | solution.py:389
  59.7 1.0 copy-start.9
  77.3 1.7 copy-start.3
  79.0 26.2 %copy-start.4 = (bf16[2,256,512]{2,1,0:T(8,128)(2,1)S(1)}, bf16[2,256,512]{2,1,0:T(8,128)(2,1)}, u32[]{:S(2)}) copy-start(bf16[2,256,512]{2,1,0:T(8,128)(2,1)} %get-tuple-element.69.refs_3_) | copy-start | bytes 1572868
  79.0 13.6 %collective-permute-start.6 = (bf16[2,256,512]{2,1,0:T(8,128)(2,1)}, bf16[2,256,512]{2,1,0:T(8,128)(2,1)S(1)}, u32[]{:S(2)}, u32[]{:S(2)}) collective-permute-start(bf16[2,256,512]{2,1,0:T(8,128)(2,1)} %get-tuple-element.70), channel_id=1, source_target_pairs={{0,2},{1,3},{2,4},{3,5},{4,6},{5,7},{6,0},{7,1},{8,10},{9,11},{10,... | collective-permute-start | bytes 1572872 | tf_op jit(solution)/shard_map/ppermute | solution.py:384
  80.1 23.5 %collective-permute-start.7 = (bf16[2,256,512]{2,1,0:T(8,128)(2,1)}, bf16[2,256,512]{2,1,0:T(8,128)(2,1)S(1)}, u32[]{:S(2)}, u32[]{:S(2)}) collective-permute-start(bf16[2,256,512]{2,1,0:T(8,128)(2,1)} %get-tuple-element.71), channel_id=1, source_target_pairs={{0,4},{1,5},{2,6},{3,7},{4,0},{5,1},{6,2},{7,3},{8,12},{9,13},{10,... | collective-permute-start | bytes 1572872 | tf_op jit(solution)/shard_map/ppermute | solution.py:384
  82.3 22.9 %collective-permute-start.8 = (bf16[2,256,512]{2,1,0:T(8,128)(2,1)}, bf16[2,256,512]{2,1,0:T(8,128)(2,1)}, u32[]{:S(2)}, u32[]{:S(2)}) collective-permute-start(bf16[2,256,512]{2,1,0:T(8,128)(2,1)} %get-tuple-element.72), channel_id=1, source_target_pairs={{0,6},{1,7},{2,0},{3,1},{4,2},{5,3},{6,4},{7,5},{8,14},{9,15},{10,... | collective-permute-start | bytes 1572872 | tf_op jit(solution)/shard_map/ppermute | solution.py:384
  85.6 78.1 %all-to-all-start.2 = ((bf16[32,128,384]{2,1,0:T(8,128)(2,1)}), bf16[32,128,384]{2,1,0:T(8,128)(2,1)}, u32[]{:S(2)}, u32[]{:S(2)}) async-start(bf16[32,128,384]{2,1,0:T(8,128)(2,1)} %copy-done.3), calls=%async_computation.2 | async-start | bytes 6291456 | tf_op jit(solution)/shard_map/all_to_all | solution.py:389
  105.2 1.0 copy-start.10
  127.2 2.0 copy-start.2
  163.8 104.0 %all-to-all-start.1 = ((bf16[32,128,512]{2,1,0:T(8,128)(2,1)}), bf16[32,128,512]{2,1,0:T(8,128)(2,1)}, u32[]{:S(2)}, u32[]{:S(2)}) async-start(bf16[32,128,512]{2,1,0:T(8,128)(2,1)} %copy-done.2), calls=%async_computation.1 | async-start | bytes 8388608 | tf_op jit(solution)/shard_map/all_to_all | solution.py:389

commit v3 on v1

--- a/solution.py
+++ b/solution.py
@@ -287,20 +287,26 @@
 def place_kernel(source_ref, *refs, count, first, width):
     received_ref, out_ref, held_ref, in_sems, out_sems = refs[0], refs[-4], refs[-3], refs[-2], refs[-1]
 
+    half = BLK // 2
+
     def fetch(i):
-        return pltpu.make_async_copy(received_ref.at[source_ref[i]], held_ref.at[i], in_sems.at[i])
+        rows = pl.ds(i % 2 * half, half)
+        return pltpu.make_async_copy(
+            received_ref.at[source_ref[i // 2], rows], held_ref.at[i // 2, rows], in_sems.at[i]
+        )
 
     def store(i):
+        rows = pl.ds(i % 2 * half, half)
         return pltpu.make_async_copy(
-            held_ref.at[i], out_ref.at[pl.ds(i * BLK, BLK), pl.ds(first, width)], out_sems.at[i]
+            held_ref.at[i // 2, rows], out_ref.at[pl.ds(i * half, half), pl.ds(first, width)], out_sems.at[i]
         )
 
-    for i in range(count):
+    for i in range(2 * count):
         fetch(i).start()
-    for i in range(count):
+    for i in range(2 * count):
         fetch(i).wait()
         store(i).start()
-    for i in range(count):
+    for i in range(2 * count):
         store(i).wait()
 
 
@@ -314,8 +320,8 @@
         out_shape=jax.ShapeDtypeStruct((count * BLK, full_width), jnp.bfloat16),
         scratch_shapes=[
             pltpu.VMEM((count, BLK, width), jnp.bfloat16),
-            pltpu.SemaphoreType.DMA((count,)),
-            pltpu.SemaphoreType.DMA((count,)),
+            pltpu.SemaphoreType.DMA((2 * count,)),
+            pltpu.SemaphoreType.DMA((2 * count,)),
         ],
         input_output_aliases={} if result is None else {2: 0},
         compiler_params=pltpu.CompilerParams(vmem_limit_bytes=SHARED_VMEM_BYTES),

time: 267 us -> 268 us (level)
  transfers between devices with their start and end apart: 8 -> 8, of which waited for: 7 -> 7; matrix products, arithmetic and copies ran while one was open for 1% -> 1% of each run, Pallas kernels for 16% -> 17%
where the time goes in v3:
time: 268 us; the launch traced here: 267 us
  waiting for transfers between devices  180 us (67%)
  Pallas kernels  51.6 us (19%)
  starting transfers between devices  30.7 us (11%)
  local copies, waits for them, and re-layouts  3.51 us (1%)
    all_to_all x2, waiting for transfers between devices, shards(): lax.all_to_all(sent, 'ctx', split_axis=0, concat_axis=0, tiled=True)  152 us
    pallas_call x3, Pallas kernels, attend(): pl.pallas_call(functools.partial(attend_kernel, heads=heads, count=count,...  36.1 us
    all_to_all x2, starting transfers between devices, shards(): lax.all_to_all(sent, 'ctx', split_axis=0, concat_axis=0, tiled=True)  19 us
    all_to_all x1, waiting for transfers between devices, shards(): lax.all_to_all(opening, 'head', split_axis=0, concat_axis=0, tiled=True)  16.1 us
    ppermute x3, waiting for transfers between devices, shards(): sources.append(lax.ppermute(part, 'head', onward) if step else part)  8.37 us
    pallas_call x2, Pallas kernels, place(): pl.pallas_call(functools.partial(place_kernel, count=count, first=first,...  6.96 us
  transfers between devices with their start and end apart: 8, of which 7 were waited for; matrix products, arithmetic and copies ran while one was open for 1% of the time, Pallas kernels for 17%

profile of v3, /device:TPU:33, one launch (start us, length us, event | category | flops | bytes accessed | tf_op | source)
XLA Modules:
  0.0 267.2 jit_solution(1691617362373372590)
XLA Ops:
  0.0 2.6 first_parts.1
  2.6 5.2 %all-to-all-start = ((bf16[8,256,512]{2,1,0:T(8,128)(2,1)}), bf16[8,256,512]{2,1,0:T(8,128)(2,1)S(1)}, u32[]{:S(2)}, u32[]{:S(2)}) async-start(bf16[8,256,512]{2,1,0:T(8,128)(2,1)} %first_parts.1), calls=%async_computation | async-start | bytes 4194304 | tf_op jit(solution)/shard_map/all_to_all | solution.py:351
  7.8 0.6 pad_add_fusion.place_ref
  8.4 0.0 copy-start.8
  8.4 3.6 %later_parts.1 = (bf16[2,256,768]{2,1,0:T(8,128)(2,1)}, bf16[2,256,768]{2,1,0:T(8,128)(2,1)}, bf16[2,256,768]{2,1,0:T(8,128)(2,1)}, bf16[2,256,768]{2,1,0:T(8,128)(2,1)}, bf16[4,256,768]{2,1,0:T(8,128)(2,1)}) custom-call(s32[2]{0:T(128)} %pad_add_fusion.place_ref, bf16[256,8192]{1,0:T(8,128)(2,1)} %q_ref.3), custom_call_target="tpu_custom_call" | custom-call | bytes 8388608 | tf_op jit(solution)/shard_map/later_parts/pallas_call | solution.py:243
  12.0 0.1 collective-permute-start
  12.1 0.0 copy-done.8
  12.1 0.1 and_select_fusion.6
  12.2 0.8 select_reduce_fusion.slot_ref
  13.0 2.9 %collective-permute-done.got_ref = bf16[4,256,768]{2,1,0:T(8,128)(2,1)} collective-permute-done((bf16[4,256,768]{2,1,0:T(8,128)(2,1)}, bf16[4,256,768]{2,1,0:T(8,128)(2,1)}, u32[]{:S(2)}, u32[]{:S(2)}) %collective-permute-start) | collective-permute-done | bytes 1572896 | tf_op jit(solution)/shard_map/ppermute | solution.py:350
  15.8 2.2 fill.1
  18.1 16.1 %all-to-all-done = bf16[8,256,512]{2,1,0:T(8,128)(2,1)S(1)} async-done(((bf16[8,256,512]{2,1,0:T(8,128)(2,1)}), bf16[8,256,512]{2,1,0:T(8,128)(2,1)S(1)}, u32[]{:S(2)}, u32[]{:S(2)}) %all-to-all-start) | async-done | bytes 2097184 | tf_op jit(solution)/shard_map/all_to_all | solution.py:351
  34.1 0.0 copy-start
  34.2 3.5 %collective-permute-start.1 = (bf16[896,256]{1,0:T(8,128)(2,1)S(1)}, bf16[896,256]{1,0:T(8,128)(2,1)S(1)}, u32[]{:S(2)}, u32[]{:S(2)}) collective-permute-start(bf16[896,256]{1,0:T(8,128)(2,1)S(1)} %slice.4), channel_id=1, source_target_pairs={{0,8},{8,16},{16,24},{24,32},{32,40},{40,48},{48,56},{56,64},{64,7... | collective-permute-start | bytes 1376264 | tf_op jit(solution)/shard_map/ppermute | solution.py:368
  37.7 0.4 collective-permute-start.2
  38.1 1.8 collective-permute-start.3
  39.9 0.7 collective-permute-start.4
  40.6 0.0 copy-done
  40.6 6.0 %attend.4.refs_2_ = bf16[32,128,256]{2,1,0:T(8,128)(2,1)} custom-call(s32[512]{0:T(512)} %doc_ref.5, s32[16]{0:T(128)} %select_reduce_fusion.slot_ref, s32[1]{0:T(128)} %bitcast.2.shard_ref, bf16[2048,512]{1,0:T(8,128)(2,1)} %bitcast.5), custom_call_target="tpu_custom_call" | custom-call | tf_op jit(solution)/shard_map/attend/pallas_call | solution.py:134
  46.6 0.7 collective-permute-done.1.refs_2_.refs_1_
  47.3 0.0 copy-start.6
  47.3 0.8 copy-done.6
  48.1 5.9 %attend.5 = bf16[32,128,256]{2,1,0:T(8,128)(2,1)} custom-call(s32[512]{0:T(512)} %doc_ref.5, s32[16]{0:T(128)} %select_reduce_fusion.slot_ref, s32[1]{0:T(128)} %bitcast.2.shard_ref, bf16[2048,512]{1,0:T(8,128)(2,1)} %bitcast.6, bf16[896,256]{1,0:T(8,128)(2,1)} %copy-done.6, bf16[32,128,256]{2,1,0:T(8,128)(2,1)} %attend.4.refs_2_), custom_call_target="tpu_custom_call", output_to_operand_aliasing={{}: (5, {})} | custom-call | flops 999999995904 | tf_op jit(solution)/shard_map/attend/pallas_call | solution.py:134
  54.0 0.0 copy-start.1
  54.0 0.0 copy-start.3
  54.0 0.0 copy-start.4
  54.0 0.0 copy-start.5
  54.0 0.0 copy-start.7
  54.0 12.4 %all-to-all-start.2 = ((bf16[32,128,256]{2,1,0:T(8,128)(2,1)}), bf16[32,128,256]{2,1,0:T(8,128)(2,1)}, u32[]{:S(2)}, u32[]{:S(2)}) async-start(bf16[32,128,256]{2,1,0:T(8,128)(2,1)} %attend.5), calls=%async_computation.2 | async-start | bytes 4194304 | tf_op jit(solution)/shard_map/all_to_all | solution.py:392
  66.4 0.0 collective-permute-done.2.refs_4_
  66.5 7.1 %collective-permute-done.3.refs_5_ = bf16[2,256,768]{2,1,0:T(8,128)(2,1)} collective-permute-done((bf16[2,256,768]{2,1,0:T(8,128)(2,1)}, bf16[2,256,768]{2,1,0:T(8,128)(2,1)}, u32[]{:S(2)}, u32[]{:S(2)}) %collective-permute-start.3) | collective-permute-done | bytes 786464 | tf_op jit(solution)/shard_map/ppermute | solution.py:387
  73.5 1.3 collective-permute-done.4.refs_6_
  74.8 0.0 copy-done.1
  74.8 0.0 copy-done.3
  74.8 0.0 copy-done.4
  74.8 0.0 copy-done.5
  74.8 0.0 copy-done.7
  74.8 24.2 %attend.3 = bf16[32,128,768]{2,1,0:T(8,128)(2,1)S(1)} custom-call(s32[512]{0:T(512)S(1)} %copy-done.4, s32[16]{0:T(128)S(1)} %copy-done.5, s32[1]{0:T(128)} %bitcast.2.shard_ref, s32[16]{0:T(128)S(1)} %get-tuple-element.33.refs_0_, bf16[2048,512]{1,0:T(8,128)(2,1)S(1)} %bitcast.7, bf16[896,256]{1,0:T(8,128)(2,1)S(1)} %copy-done.7, ...), custom_call_target="tpu_custom_call" | custom-call | flops 999999995904 | tf_op jit(solution)/shard_map/attend/pallas_call | solution.py:134
  99.1 0.0 copy-start.2
  99.1 2.7 copy-done.2
  101.8 13.8 %all-to-all-done.2.refs_0_ = bf16[32,128,256]{2,1,0:T(8,128)(2,1)} async-done(((bf16[32,128,256]{2,1,0:T(8,128)(2,1)}), bf16[32,128,256]{2,1,0:T(8,128)(2,1)}, u32[]{:S(2)}, u32[]{:S(2)}) %all-to-all-start.2) | async-done | bytes 2097184 | tf_op jit(solution)/shard_map/all_to_all | solution.py:392
  115.6 6.6 %all-to-all-start.1 = ((bf16[32,128,768]{2,1,0:T(8,128)(2,1)}), bf16[32,128,768]{2,1,0:T(8,128)(2,1)}, u32[]{:S(2)}, u32[]{:S(2)}) async-start(bf16[32,128,768]{2,1,0:T(8,128)(2,1)} %copy-done.2), calls=%async_computation.1 | async-start | bytes 12582912 | tf_op jit(solution)/shard_map/all_to_all | solution.py:392
  122.2 2.9 %place.2.refs_1_ = bf16[2048,1024]{1,0:T(8,128)(2,1)} custom-call(s32[16]{0:T(128)S(1)} %get-tuple-element.31.source_ref, bf16[32,128,256]{2,1,0:T(8,128)(2,1)} %all-to-all-done.2.refs_0_), custom_call_target="tpu_custom_call" | custom-call | bytes 2097152 | tf_op jit(solution)/shard_map/place/pallas_call | solution.py:316
  125.1 137.9 %all-to-all-done.1.refs_0_ = bf16[32,128,768]{2,1,0:T(8,128)(2,1)} async-done(((bf16[32,128,768]{2,1,0:T(8,128)(2,1)}), bf16[32,128,768]{2,1,0:T(8,128)(2,1)}, u32[]{:S(2)}, u32[]{:S(2)}) %all-to-all-start.1) | async-done | bytes 6291488 | tf_op jit(solution)/shard_map/all_to_all | solution.py:392
  263.0 4.1 %place.3 = bf16[2048,1024]{1,0:T(8,128)(2,1)} custom-call(s32[16]{0:T(128)S(1)} %get-tuple-element.31.source_ref, bf16[32,128,768]{2,1,0:T(8,128)(2,1)} %all-to-all-done.1.refs_0_, bf16[2048,1024]{1,0:T(8,128)(2,1)} %place.2.refs_1_), custom_call_target="tpu_custom_call", output_to_operand_aliasing={{}: (2, {})} | custom-call | bytes 6291456 | tf_op jit(solution)/shard_map/place/pallas_call | solution.py:316
  (3 shorter events, 0.0 us)
Async XLA Ops:
  2.6 31.5 %all-to-all-start = ((bf16[8,256,512]{2,1,0:T(8,128)(2,1)}), bf16[8,256,512]{2,1,0:T(8,128)(2,1)S(1)}, u32[]{:S(2)}, u32[]{:S(2)}) async-start(bf16[8,256,512]{2,1,0:T(8,128)(2,1)} %first_parts.1), calls=%async_computation | async-start | bytes 4194304 | tf_op jit(solution)/shard_map/all_to_all | solution.py:351
  8.4 3.7 %copy-start.8 = (s32[512]{0:T(512)S(1)}, s32[512]{0:T(512)}, u32[]{:S(2)}) copy-start(s32[512]{0:T(512)} %param.9) | copy-start | bytes 6148
  12.0 3.8 %collective-permute-start = (bf16[4,256,768]{2,1,0:T(8,128)(2,1)}, bf16[4,256,768]{2,1,0:T(8,128)(2,1)}, u32[]{:S(2)}, u32[]{:S(2)}) collective-permute-start(bf16[4,256,768]{2,1,0:T(8,128)(2,1)} %get-tuple-element.22), channel_id=1, source_target_pairs={{0,1},{1,0},{2,3},{3,2},{4,5},{5,4},{6,7},{7,6},{8,9},{9,8},{10,11... | collective-permute-start | bytes 4718600 | tf_op jit(solution)/shard_map/ppermute | solution.py:350
  34.1 6.4 %copy-start = (bf16[8,256,512]{2,1,0:T(8,128)(2,1)}, bf16[8,256,512]{2,1,0:T(8,128)(2,1)S(1)}, u32[]{:S(2)}) copy-start(bf16[8,256,512]{2,1,0:T(8,128)(2,1)S(1)} %all-to-all-done) | copy-start | bytes 6291460
  34.2 13.2 %collective-permute-start.1 = (bf16[896,256]{1,0:T(8,128)(2,1)S(1)}, bf16[896,256]{1,0:T(8,128)(2,1)S(1)}, u32[]{:S(2)}, u32[]{:S(2)}) collective-permute-start(bf16[896,256]{1,0:T(8,128)(2,1)S(1)} %slice.4), channel_id=1, source_target_pairs={{0,8},{8,16},{16,24},{24,32},{32,40},{40,48},{48,56},{56,64},{64,7... | collective-permute-start | bytes 1376264 | tf_op jit(solution)/shard_map/ppermute | solution.py:368
  37.7 28.7 %collective-permute-start.2 = (bf16[2,256,768]{2,1,0:T(8,128)(2,1)}, bf16[2,256,768]{2,1,0:T(8,128)(2,1)}, u32[]{:S(2)}, u32[]{:S(2)}) collective-permute-start(bf16[2,256,768]{2,1,0:T(8,128)(2,1)} %get-tuple-element.36), channel_id=1, source_target_pairs={{0,2},{1,3},{2,4},{3,5},{4,6},{5,7},{6,0},{7,1},{8,10},{9,11},{10,... | collective-permute-start | bytes 2359304 | tf_op jit(solution)/shard_map/ppermute | solution.py:387
  38.1 35.4 %collective-permute-start.3 = (bf16[2,256,768]{2,1,0:T(8,128)(2,1)}, bf16[2,256,768]{2,1,0:T(8,128)(2,1)}, u32[]{:S(2)}, u32[]{:S(2)}) collective-permute-start(bf16[2,256,768]{2,1,0:T(8,128)(2,1)} %get-tuple-element.37), channel_id=1, source_target_pairs={{0,4},{1,5},{2,6},{3,7},{4,0},{5,1},{6,2},{7,3},{8,12},{9,13},{10,... | collective-permute-start | bytes 2359304 | tf_op jit(solution)/shard_map/ppermute | solution.py:387
  39.9 34.9 %collective-permute-start.4 = (bf16[2,256,768]{2,1,0:T(8,128)(2,1)}, bf16[2,256,768]{2,1,0:T(8,128)(2,1)}, u32[]{:S(2)}, u32[]{:S(2)}) collective-permute-start(bf16[2,256,768]{2,1,0:T(8,128)(2,1)} %get-tuple-element.38), channel_id=1, source_target_pairs={{0,6},{1,7},{2,0},{3,1},{4,2},{5,3},{6,4},{7,5},{8,14},{9,15},{10,... | collective-permute-start | bytes 2359304 | tf_op jit(solution)/shard_map/ppermute | solution.py:387
  47.3 0.8 copy-start.6
  54.0 20.8 %copy-start.1 = (bf16[8,256,512]{2,1,0:T(8,128)(2,1)S(1)}, bf16[8,256,512]{2,1,0:T(8,128)(2,1)}, u32[]{:S(2)}) copy-start(bf16[8,256,512]{2,1,0:T(8,128)(2,1)} %copy-done) | copy-start | bytes 6291460
  54.0 20.8 %copy-start.3 = (bf16[2,256,768]{2,1,0:T(8,128)(2,1)S(1)}, bf16[2,256,768]{2,1,0:T(8,128)(2,1)}, u32[]{:S(2)}) copy-start(bf16[2,256,768]{2,1,0:T(8,128)(2,1)} %get-tuple-element.35.refs_3_) | copy-start | bytes 2359300
  54.0 20.8 %copy-start.4 = (s32[512]{0:T(512)S(1)}, s32[512]{0:T(512)}, u32[]{:S(2)}) copy-start(s32[512]{0:T(512)} %doc_ref.5) | copy-start | bytes 6148
  54.0 20.8 %copy-start.5 = (s32[16]{0:T(128)S(1)}, s32[16]{0:T(128)}, u32[]{:S(2)}) copy-start(s32[16]{0:T(128)} %select_reduce_fusion.slot_ref) | copy-start | bytes 196
  54.0 20.8 %copy-start.7 = (bf16[896,256]{1,0:T(8,128)(2,1)S(1)}, bf16[896,256]{1,0:T(8,128)(2,1)}, u32[]{:S(2)}) copy-start(bf16[896,256]{1,0:T(8,128)(2,1)} %copy-done.6) | copy-start | bytes 1376260
  54.0 61.5 %all-to-all-start.2 = ((bf16[32,128,256]{2,1,0:T(8,128)(2,1)}), bf16[32,128,256]{2,1,0:T(8,128)(2,1)}, u32[]{:S(2)}, u32[]{:S(2)}) async-start(bf16[32,128,256]{2,1,0:T(8,128)(2,1)} %attend.5), calls=%async_computation.2 | async-start | bytes 4194304 | tf_op jit(solution)/shard_map/all_to_all | solution.py:392
  99.1 2.7 copy-start.2
  115.6 147.4 %all-to-all-start.1 = ((bf16[32,128,768]{2,1,0:T(8,128)(2,1)}), bf16[32,128,768]{2,1,0:T(8,128)(2,1)}, u32[]{:S(2)}, u32[]{:S(2)}) async-start(bf16[32,128,768]{2,1,0:T(8,128)(2,1)} %copy-done.2), calls=%async_computation.1 | async-start | bytes 12582912 | tf_op jit(solution)/shard_map/all_to_all | solution.py:392
